TPU v7x, 512 devices: a whole 4x4x16 slice. The times are simulated.
512 devices in a mesh: expert: 64 (over y, x, z_hi, core), fsdp: 8 (over z_lo).
Axes of the slice: x: 4, y: 4, z: 16 (z_hi: 2, z_lo: 8; z = z_hi * 8 + z_lo), core: 2. Of those that a mesh axis runs over, the one named last changes fastest.
Arguments:
- tokens: bfloat16 [768, 4096], P('expert', 'fsdp'), may hold values from -6 to 6
- gain: float32 [4096], P('fsdp'), may hold values from 0.1 to 1.9
- w_sel: bfloat16 [4096, 64], P('fsdp'), may hold values from -0.09375 to 0.09375
- w_up: bfloat16 [64, 4096, 1024], P('expert', 'fsdp'), may hold values from -0.09375 to 0.09375
- w_down: bfloat16 [64, 1024, 4096], P('expert', None, 'fsdp'), may hold values from -0.1875 to 0.1875
- routes: int32 [2, 768, 8], P(None, 'expert'), may hold values from 0 to 63, all different within a row; in each aligned block of 12 rows (0 to 11, 12 to 23, ..., all dimensions but the last counted through in order) at most 3 rows name the same one
- cotangent: bfloat16 [768, 4096], P('expert', 'fsdp'), may hold values from -6 to 6
Outputs:
- mixed: bfloat16 [768, 4096], P('expert', 'fsdp')
- d_tokens: bfloat16 [768, 4096], P('expert', 'fsdp')
- d_w_up: bfloat16 [64, 4096, 1024], P('expert', 'fsdp')
- d_w_down: bfloat16 [64, 1024, 4096], P('expert', None, 'fsdp')
- d_w_sel: float32 [4096, 64], P('fsdp')
Inputs may be any that keep to these rules, and one draw needn't show every extreme that they name: `routes`: each token names 8 different experts in each loop; in each loop each aligned block of 12 tokens names any one expert at most 3 times, and some block names some expert exactly 3 times.
All inputs are finite; a program needn't handle non-finite values.
Results may differ from a plain program's by a relative error of at most 0.019.
Values may be sent and summed in bfloat16 or wider, within the bound.
A program may use at most 64 MiB of HBM per device.

v0:
```python
import jax
import jax.numpy as jnp
from jax import lax
from jax.sharding import PartitionSpec as P

EPSILON = 1e-06
HIGHEST = lax.Precision.HIGHEST


def local_placer(route_rows, experts, capacity):
    flat = route_rows.reshape(-1)
    marks = (flat[:, None] == jnp.arange(experts, dtype=jnp.int32)[None, :]).astype(jnp.int32)
    earlier = jnp.cumsum(marks, axis=0) - marks
    slots = jnp.sum(earlier * marks, axis=1)
    target = flat * capacity + slots
    return (target[None, :] == jnp.arange(experts * capacity, dtype=jnp.int32)[:, None]).astype(
        jnp.bfloat16
    )


def send_rows(token_rows, placer, experts, capacity):
    local_width = token_rows.shape[1]
    packed = jnp.dot(placer, token_rows, preferred_element_type=jnp.float32).astype(jnp.bfloat16)
    arrived = lax.all_to_all(
        packed.reshape(experts, capacity, local_width),
        "expert",
        split_axis=0,
        concat_axis=0,
        tiled=True,
    )
    return arrived.reshape(experts * capacity, local_width)


def return_rows(expert_rows, placer, experts, capacity):
    local_width = expert_rows.shape[1]
    returned = lax.all_to_all(
        expert_rows.reshape(experts, capacity, local_width),
        "expert",
        split_axis=0,
        concat_axis=0,
        tiled=True,
    )
    flat = returned.reshape(experts * capacity, local_width)
    return jnp.einsum("sa,sd->ad", placer, flat, preferred_element_type=jnp.float32).astype(
        jnp.bfloat16
    )


def silu_slope(pre):
    sig = jax.nn.sigmoid(pre)
    return sig * (1.0 + pre * (1.0 - sig))


def hidden_sum(term, saved_pre, hidden_width):
    total = lax.psum(term(0, hidden_width), "fsdp")
    if saved_pre is None:
        return ((total * jax.nn.sigmoid(total)).astype(jnp.bfloat16), total)
    return ((total * silu_slope(saved_pre)).astype(jnp.bfloat16), None)


def shards(tokens, gain, w_sel, w_up, w_down, routes, cotangent):
    experts = lax.axis_size("expert")
    group_size, local_width = tokens.shape
    top_count = routes.shape[2]
    loop_count = routes.shape[0]
    capacity = 2 * group_size * top_count // experts
    hidden_width = w_up.shape[2]
    model_width = local_width * lax.axis_size("fsdp")
    up_proj = w_up[0]
    down_proj = w_down[0]
    expert_ids = jnp.arange(w_sel.shape[1], dtype=jnp.int32)
    current = tokens
    saved = []
    for loop_index in range(loop_count):
        widened = current.astype(jnp.float32)
        squares = lax.psum(jnp.sum(widened * widened, axis=1), "fsdp")
        inv_rms = lax.rsqrt(squares / model_width + EPSILON)
        normed = (widened * inv_rms[:, None] * gain[None, :]).astype(jnp.bfloat16)
        logits = lax.psum(jnp.dot(normed, w_sel, preferred_element_type=jnp.float32), "fsdp")
        chooser = (routes[loop_index][:, :, None] == expert_ids[None, None, :]).astype(jnp.float32)
        gates = jax.nn.sigmoid(jnp.sum(chooser * logits[:, None, :], axis=2))
        placer = local_placer(routes[loop_index], experts, capacity)
        arrived = send_rows(jnp.repeat(normed, top_count, axis=0), placer, experts, capacity)

        def forward_term(start, count):
            return jnp.einsum("dh,rd->hr", up_proj, arrived, preferred_element_type=jnp.float32)

        hidden, pre_kept = hidden_sum(forward_term, None, hidden_width)
        outputs = jnp.einsum(
            "hr,hd->rd", hidden, down_proj, preferred_element_type=jnp.float32
        ).astype(jnp.bfloat16)
        back = return_rows(outputs, placer, experts, capacity).reshape(
            group_size, top_count, local_width
        )
        blend = jnp.sum(gates[:, :, None] * back.astype(jnp.float32), axis=1)
        saved.append(
            (current, inv_rms, normed, gates, chooser, placer, arrived, hidden, pre_kept, back)
        )
        current = (widened + blend).astype(jnp.bfloat16)
    mixed = current
    incoming = cotangent
    up_total = jnp.zeros(up_proj.shape, jnp.float32)
    down_total = jnp.zeros(down_proj.shape, jnp.float32)
    select_total = jnp.zeros(w_sel.shape, jnp.float32)
    for loop_index in reversed(range(loop_count)):
        current, inv_rms, normed, gates, chooser, placer, arrived, hidden, pre_kept, back = saved[
            loop_index
        ]
        grad_wide = incoming.astype(jnp.float32)
        gate_grad = lax.psum(
            jnp.sum(grad_wide[:, None, :] * back.astype(jnp.float32), axis=2), "fsdp"
        )
        out_grad = (
            (gates[:, :, None] * grad_wide[:, None, :])
            .astype(jnp.bfloat16)
            .reshape(group_size * top_count, local_width)
        )
        grad_rows = send_rows(out_grad, placer, experts, capacity)

        def backward_term(start, count):
            return jnp.einsum("hd,rd->hr", down_proj, grad_rows, preferred_element_type=jnp.float32)

        hidden_grad, unused = hidden_sum(backward_term, pre_kept, hidden_width)
        down_total = down_total + jnp.einsum(
            "hr,rd->hd", hidden, grad_rows, preferred_element_type=jnp.float32
        )
        up_total = up_total + jnp.einsum(
            "rd,hr->dh", arrived, hidden_grad, preferred_element_type=jnp.float32
        )
        back_grad = jnp.einsum(
            "hr,dh->rd", hidden_grad, up_proj, preferred_element_type=jnp.float32
        ).astype(jnp.bfloat16)
        back_rows = return_rows(back_grad, placer, experts, capacity).reshape(
            group_size, top_count, local_width
        )
        logit_grad = gate_grad * gates * (1.0 - gates)
        logit_table = jnp.sum(chooser * logit_grad[:, :, None], axis=1)
        normed_grad = jnp.sum(back_rows.astype(jnp.float32), axis=1) + jnp.dot(
            logit_table, w_sel.astype(jnp.float32).T, precision=HIGHEST
        )
        select_total = select_total + jnp.dot(
            normed.astype(jnp.float32).T, logit_table, precision=HIGHEST
        )
        widened = current.astype(jnp.float32)
        inner_sum = lax.psum(jnp.sum(widened * gain[None, :] * normed_grad, axis=1), "fsdp")
        cube = inv_rms * inv_rms * inv_rms / model_width
        new_grad = (
            grad_wide
            + inv_rms[:, None] * gain[None, :] * normed_grad
            - cube[:, None] * widened * inner_sum[:, None]
        )
        incoming = new_grad.astype(jnp.bfloat16)
    select_grad = lax.psum(select_total, "expert")
    return (
        mixed,
        incoming,
        up_total.astype(jnp.bfloat16)[None],
        down_total.astype(jnp.bfloat16)[None],
        select_grad,
    )


def solution(mesh):
    placed = (
        P("expert", "fsdp"),
        P("fsdp"),
        P("fsdp", None),
        P("expert", "fsdp", None),
        P("expert", None, "fsdp"),
        P(None, "expert", None),
        P("expert", "fsdp"),
    )
    return jax.shard_map(
        shards,
        mesh=mesh,
        in_specs=placed,
        out_specs=(
            P("expert", "fsdp"),
            P("expert", "fsdp"),
            P("expert", "fsdp", None),
            P("expert", None, "fsdp"),
            P("fsdp", None),
        ),
        check_vma=False,
    )
```

profile of v0, /device:TPU:1, one launch (start us, length us, event | category | flops | bytes accessed | tf_op | source)
XLA Modules:
  0.0 1919.1 jit_solution(11362208735708970300)
XLA Ops:
  8.2 33.3 %psum.91 = f32[12]{0:T(128)S(1)} all-reduce(f32[12]{0:T(128)S(1)} %fusion.44), channel_id=1, replica_groups=mesh['expert'=64,'fsdp'=8] {'fsdp'}, use_global_device_ids=true, to_apply=%region_1.0 | all-reduce | flops 12 | bytes 96 | tf_op jit(solution)/shard_map/psum | solution.py:76
  44.5 36.2 %all_to_all.40 = bf16[64,3,512]{2,1,0:T(4,128)(2,1)S(1)} all-to-all(bf16[64,3,512]{2,1,0:T(4,128)(2,1)S(1)} %reshape.148), channel_id=1, replica_groups=mesh['expert'=64,'fsdp'=8] {'expert'}, dimensions={0} | all-to-all | bytes 393216 | tf_op jit(solution)/shard_map/all_to_all | solution.py:24
  82.5 112.0 %all-reduce.7.cloned.1.call-done = f32[1024,192]{0,1:T(8,128)} async-done(((f32[1024,192]{0,1:T(8,128)}), f32[1024,192]{0,1:T(8,128)}) %all-reduce.7.cloned.1.call-update) | async-done | bytes 786448 | tf_op jit(solution)/shard_map/psum | solution.py:55
  196.8 15.9 all-to-all-start.1
  213.0 30.5 %psum.92 = f32[12,64]{1,0:T(8,128)S(1)} all-reduce(f32[12,64]{1,0:T(8,128)S(1)} %fusion.67), channel_id=1, replica_groups=mesh['expert'=64,'fsdp'=8] {'fsdp'}, use_global_device_ids=true, to_apply=%region_2.0 | all-reduce | flops 768 | bytes 6144 | tf_op jit(solution)/shard_map/psum | solution.py:79
  245.2 21.6 %psum.94 = f32[12]{0:T(128)S(1)} all-reduce(f32[12]{0:T(128)S(1)} %get-tuple-element.7), channel_id=1, replica_groups=mesh['expert'=64,'fsdp'=8] {'fsdp'}, use_global_device_ids=true, to_apply=%region_9.10 | all-reduce | flops 12 | bytes 96 | tf_op jit(solution)/shard_map/psum | solution.py:76
  267.7 42.5 %all_to_all.41 = bf16[64,3,512]{2,1,0:T(4,128)(2,1)S(1)} all-to-all(bf16[64,3,512]{2,1,0:T(4,128)(2,1)S(1)} %reshape.153), channel_id=1, replica_groups=mesh['expert'=64,'fsdp'=8] {'expert'}, dimensions={0} | all-to-all | bytes 393216 | tf_op jit(solution)/shard_map/all_to_all | solution.py:24
  311.7 112.8 %all-reduce.9.cloned.1.call-done = f32[1024,192]{0,1:T(8,128)} async-done(((f32[1024,192]{0,1:T(8,128)}), f32[1024,192]{0,1:T(8,128)}) %all-reduce.9.cloned.1.call-update) | async-done | bytes 786448 | tf_op jit(solution)/shard_map/psum | solution.py:55
  426.9 15.9 all-to-all-start.3
  443.1 18.4 all-to-all-done.3
  462.1 49.7 %all-reduce = (f32[12,64]{1,0:T(8,128)S(1)}, f32[12,8]{1,0:T(8,128)S(1)}) all-reduce(f32[12,64]{1,0:T(8,128)S(1)} %fusion.68, f32[12,8]{1,0:T(8,128)S(1)} %reduce_sum.158), channel_id=1, replica_groups=mesh['expert'=64,'fsdp'=8] {'fsdp'}, use_global_device_ids=true, to_apply=%region_10.11 | all-reduce | flops 864 | bytes 6912 | tf_op jit(solution)/shard_map/psum | solution.py:79
  512.4 36.2 %all_to_all.42 = bf16[64,3,512]{2,1,0:T(4,128)(2,1)S(1)} all-to-all(bf16[64,3,512]{2,1,0:T(4,128)(2,1)S(1)} %reshape.157), channel_id=1, replica_groups=mesh['expert'=64,'fsdp'=8] {'expert'}, dimensions={0} | all-to-all | bytes 393216 | tf_op jit(solution)/shard_map/all_to_all | solution.py:24
  550.2 109.7 %all-reduce.11.cloned.1.call-done = f32[1024,192]{0,1:T(8,128)} async-done(((f32[1024,192]{0,1:T(8,128)}), f32[1024,192]{0,1:T(8,128)}) %all-reduce.11.cloned.1.call-update) | async-done | bytes 786448 | tf_op jit(solution)/shard_map/psum | solution.py:55
  662.9 15.9 all-to-all-start.5
  679.6 17.9 all-to-all-done.5
  698.8 29.5 %psum.99 = f32[12]{0:T(128)S(1)} all-reduce(f32[12]{0:T(128)S(1)} %get-tuple-element.25), channel_id=1, replica_groups=mesh['expert'=64,'fsdp'=8] {'fsdp'}, use_global_device_ids=true, to_apply=%region_22.23 | all-reduce | flops 12 | bytes 96 | tf_op jit(solution)/shard_map/psum | solution.py:145
  731.3 13.6 all-to-all-start.6
  745.9 18.4 all-to-all-done.6
  772.4 23.3 %psum.101 = f32[12,8]{1,0:T(8,128)S(1)} all-reduce(f32[12,8]{1,0:T(8,128)S(1)} %reduce_sum.163), channel_id=1, replica_groups=mesh['expert'=64,'fsdp'=8] {'fsdp'}, use_global_device_ids=true, to_apply=%region_26.27 | all-reduce | flops 96 | bytes 768 | tf_op jit(solution)/shard_map/psum | solution.py:110
  795.7 81.5 %all-reduce.13.cloned.1.call-done = f32[1024,192]{0,1:T(8,128)} async-done(((f32[1024,192]{0,1:T(8,128)}), f32[1024,192]{0,1:T(8,128)}) %all-reduce.13.cloned.1.call-update) | async-done | bytes 786448 | tf_op jit(solution)/shard_map/psum | solution.py:55
  880.2 15.9 all-to-all-start.7
  902.2 12.7 all-to-all-done.7
  915.5 29.9 %psum.102 = f32[12]{0:T(128)S(1)} all-reduce(f32[12]{0:T(128)S(1)} %get-tuple-element.27), channel_id=1, replica_groups=mesh['expert'=64,'fsdp'=8] {'fsdp'}, use_global_device_ids=true, to_apply=%region_29.30 | all-reduce | flops 12 | bytes 96 | tf_op jit(solution)/shard_map/psum | solution.py:145
  946.1 964.9 %all-reduce.15.cloned.1.call-done = f32[512,64]{0,1:T(8,128)} async-done(((f32[512,64]{0,1:T(8,128)}), f32[512,64]{0,1:T(8,128)}) %all-reduce.15.cloned.1.call-update) | async-done | bytes 131088 | tf_op jit(solution)/shard_map/psum | solution.py:153
  (139 shorter events, 46.7 us)
Async XLA Ops:
  7.2 187.3 %copy-start = (bf16[1,1024,512]{2,1,0:T(8,128)(2,1)S(1)}, bf16[1,1024,512]{2,1,0:T(8,128)(2,1)}, u32[]{:S(2)}) copy-start(bf16[1,1024,512]{2,1,0:T(8,128)(2,1)} %param.11) | copy-start | bytes 3145732
  7.2 73.7 %copy-start.1 = (bf16[1,512,1024]{2,1,0:T(8,128)(2,1)S(1)}, bf16[1,512,1024]{2,1,0:T(8,128)(2,1)}, u32[]{:S(2)}) copy-start(bf16[1,512,1024]{2,1,0:T(8,128)(2,1)} %param.10) | copy-start | bytes 3145732
  7.2 187.2 %all-reduce.7.cloned.1.call-start = ((), (), s32[]{:S(2)}) async-start(), calls=%async_computation.8 | async-start | bytes 1572864 | tf_op jit(solution)/shard_map/psum | solution.py:55
  44.4 37.9 %copy-start.3 = (bf16[512,64]{0,1:T(8,128)(2,1)S(1)}, bf16[512,64]{0,1:T(8,128)(2,1)}, u32[]{:S(2)}) copy-start(bf16[512,64]{0,1:T(8,128)(2,1)} %param.9) | copy-start | bytes 196612
  195.9 49.1 %copy-start.9 = (bf16[12,512]{1,0:T(8,128)(2,1)S(1)}, bf16[12,512]{1,0:T(8,128)(2,1)}, u32[]{:S(2)}) copy-start(bf16[12,512]{1,0:T(8,128)(2,1)} %param.7) | copy-start | bytes 36868
  196.0 71.4 %copy-start.10 = (f32[512]{0:T(512)S(1)}, f32[512]{0:T(512)}, u32[]{:S(2)}) copy-start(f32[512]{0:T(512)} %param.8) | copy-start | bytes 6148
  196.8 47.2 %all-to-all-start.1 = ((bf16[64,3,512]{2,1,0:T(4,128)(2,1)}), bf16[64,3,512]{2,1,0:T(4,128)(2,1)S(1)}, u32[]{:S(2)}, u32[]{:S(2)}) async-start(bf16[64,3,512]{2,1,0:T(4,128)(2,1)} %reshape.150), calls=%async_computation.1 | async-start | bytes 524288 | tf_op jit(solution)/shard_map/all_to_all | solution.py:36
  212.7 211.9 %all-reduce.9.cloned.1.call-start = ((), (), s32[]{:S(2)}) async-start(), calls=%async_computation.9 | async-start | bytes 1572864 | tf_op jit(solution)/shard_map/psum | solution.py:55
  243.9 268.1 %copy-start.18 = (s32[96]{0:T(128)}, s32[96]{0:T(128)S(1)}, u32[]{:S(2)}) copy-start(s32[96]{0:T(128)S(1)} %multiply_add_fusion) | copy-start | bytes 1156
  267.3 44.4 %copy-start.21 = (f32[12]{0:T(128)}, f32[12]{0:T(128)S(1)}, u32[]{:S(2)}) copy-start(f32[12]{0:T(128)S(1)} %get-tuple-element.20) | copy-start | bytes 148
  311.7 131.2 %copy-start.17 = (bf16[12,512]{1,0:T(8,128)(2,1)S(1)}, bf16[12,512]{1,0:T(8,128)(2,1)}, u32[]{:S(2)}) copy-start(bf16[12,512]{1,0:T(8,128)(2,1)} %param.13) | copy-start | bytes 36868
  426.9 34.6 %all-to-all-start.3 = ((bf16[64,3,512]{2,1,0:T(4,128)(2,1)}), bf16[64,3,512]{2,1,0:T(4,128)(2,1)S(1)}, u32[]{:S(2)}, u32[]{:S(2)}) async-start(bf16[64,3,512]{2,1,0:T(4,128)(2,1)} %reshape.155), calls=%async_computation.3 | async-start | bytes 524288 | tf_op jit(solution)/shard_map/all_to_all | solution.py:36
  442.8 217.1 %all-reduce.11.cloned.1.call-start = ((), (), s32[]{:S(2)}) async-start(), calls=%async_computation.10 | async-start | bytes 1572864 | tf_op jit(solution)/shard_map/psum | solution.py:55
  511.9 38.3 %copy-start.15 = (f32[12,8]{1,0:T(8,128)}, f32[12,8]{1,0:T(8,128)S(1)}, u32[]{:S(2)}) copy-start(f32[12,8]{1,0:T(8,128)S(1)} %get-tuple-element.12) | copy-start | bytes 1156
  662.9 34.6 %all-to-all-start.5 = ((bf16[64,3,512]{2,1,0:T(4,128)(2,1)}), bf16[64,3,512]{2,1,0:T(4,128)(2,1)S(1)}, u32[]{:S(2)}, u32[]{:S(2)}) async-start(bf16[64,3,512]{2,1,0:T(4,128)(2,1)} %reshape.159), calls=%async_computation.5 | async-start | bytes 524288 | tf_op jit(solution)/shard_map/all_to_all | solution.py:36
  731.3 32.9 %all-to-all-start.6 = ((bf16[64,3,512]{2,1,0:T(4,128)(2,1)}), bf16[64,3,512]{2,1,0:T(4,128)(2,1)S(1)}, u32[]{:S(2)}, u32[]{:S(2)}) async-start(bf16[64,3,512]{2,1,0:T(4,128)(2,1)} %reshape.161), calls=%async_computation.6 | async-start | bytes 524288 | tf_op jit(solution)/shard_map/all_to_all | solution.py:24
  744.9 132.3 %all-reduce.13.cloned.1.call-start = ((), (), s32[]{:S(2)}) async-start(), calls=%async_computation.11 | async-start | bytes 1572864 | tf_op jit(solution)/shard_map/psum | solution.py:55
  795.7 100.5 %copy-start.12 = (s32[12,8]{1,0:T(8,128)S(1)}, s32[12,8]{1,0:T(8,128)}, u32[]{:S(2)}) copy-start(s32[12,8]{1,0:T(8,128)} %copy-done.11) | copy-start | bytes 1156
  795.7 100.6 %copy-start.8 = (f32[512,64]{0,1:T(8,128)S(1)}, f32[512,64]{0,1:T(8,128)}, u32[]{:S(2)}) copy-start(f32[512,64]{0,1:T(8,128)} %fusion.70) | copy-start | bytes 393220
  795.7 101.5 %copy-start.7 = (bf16[192,512]{1,0:T(8,128)(2,1)S(1)}, bf16[192,512]{1,0:T(8,128)(2,1)}, u32[]{:S(2)}) copy-start(bf16[192,512]{1,0:T(8,128)(2,1)} %reshape.162) | copy-start | bytes 589828
  880.2 34.6 %all-to-all-start.7 = ((bf16[64,3,512]{2,1,0:T(4,128)(2,1)}), bf16[64,3,512]{2,1,0:T(4,128)(2,1)S(1)}, u32[]{:S(2)}, u32[]{:S(2)}) async-start(bf16[64,3,512]{2,1,0:T(4,128)(2,1)} %reshape.163), calls=%async_computation.7 | async-start | bytes 524288 | tf_op jit(solution)/shard_map/all_to_all | solution.py:36
  896.1 1014.9 %all-reduce.15.cloned.1.call-start = ((), (), s32[]{:S(2)}) async-start(), calls=%async_computation.12 | async-start | bytes 262144 | tf_op jit(solution)/shard_map/psum | solution.py:153
  900.7 44.7 %copy-start.20 = (f32[12]{0:T(128)S(1)}, f32[12]{0:T(128)}, u32[]{:S(2)}) copy-start(f32[12]{0:T(128)} %copy-done.19) | copy-start | bytes 148
  900.7 44.7 %copy-start.22 = (f32[12]{0:T(128)S(1)}, f32[12]{0:T(128)}, u32[]{:S(2)}) copy-start(f32[12]{0:T(128)} %get-tuple-element.17) | copy-start | bytes 148
  (9 other events, 123.8 us)
Sparse Core Ops, SparseCore 0:
  82.3 112.1 all-reduce.6
  311.8 112.7 all-reduce.8
  550.3 109.5 all-reduce.10
  767.6 109.6 all-reduce.12
  900.2 1010.7 all-reduce.14
where the time goes:
time: 1920 us
  waiting for transfers between devices  1450 us (76%)
  blocking collectives  333 us (17%)
  starting transfers between devices  77.4 us (4%)
  matrix products  26.3 us (1%)
    psum x1, waiting for transfers between devices, shards(): select_grad = lax.psum(select_total, 'expert')  965 us
    psum x4, waiting for transfers between devices, hidden_sum(): total = lax.psum(term(0, hidden_width), 'fsdp')  416 us
    all_to_all x3, blocking collectives, send_rows(): lax.all_to_all(packed.reshape(experts, capacity, local_width), 'expert',...  115 us
    psum x2, blocking collectives, shards(): lax.psum(jnp.dot(normed, w_sel, preferred_element_type=jnp.float32), 'fsdp')  80.2 us
    all_to_all x4, starting transfers between devices, return_rows(): lax.all_to_all(expert_rows.reshape(experts, capacity, local_width), 'expe...  63.6 us
    psum x2, blocking collectives, shards(): lax.psum(jnp.sum(widened * gain[None, :] * normed_grad, axis=1), 'fsdp')  59.4 us
    psum x2, blocking collectives, shards(): squares = lax.psum(jnp.sum(widened * widened, axis=1), 'fsdp')  55 us
    all_to_all x4, waiting for transfers between devices, return_rows(): lax.all_to_all(expert_rows.reshape(experts, capacity, local_width), 'expe...  49 us
  transfers between devices with their start and end apart: 10, of which 9 were waited for; matrix products, arithmetic and copies ran while one was open for 1% of the time, Pallas kernels for 0%

commit v1 on v0

v1 whole, which is shorter than its diff:
```python
import functools
from types import SimpleNamespace

import jax
import jax.numpy as jnp
from jax import lax
from jax.experimental import pallas as pl
from jax.experimental.pallas import tpu as pltpu
from jax.sharding import PartitionSpec as P

EPSILON = 1e-06
HIGHEST = lax.Precision.HIGHEST
MESH = pl.DeviceIdType.MESH
BF, F32 = jnp.bfloat16, jnp.float32
PAD = 16
MARKS = 64


def iota(shape, dim):
    return lax.broadcasted_iota(jnp.int32, shape, dim)


def dot(a, b, ca, cb, precision=None):
    return lax.dot_general(
        a, b, (((ca,), (cb,)), ((), ())), precision=precision, preferred_element_type=F32
    )


def column(lanes):
    n = lanes.shape[1]
    return jnp.sum(jnp.where(iota((n, n), 0) == iota((n, n), 1), lanes, 0.0), axis=1, keepdims=True)


def two_rows(first, second):
    return jnp.where(iota(first.shape, 0) == 0, first, second)


def kernel(
    s,
    x_ref, cot_ref, gain_ref, sel_ref, up_ref, down_ref, routes_ref,
    mixed_ref, dtok_ref, dup_ref, ddown_ref, dsel_ref,
    ax, ac, a1, a2, asel,
    pbuf, rbuf, full, ebuf, gbuf,
    sb, sib, tb, rb, uf, ub, zb,
    pg, ps, pre_k, slope_k, hid_k, dh_k, rows, grads, up_acc, down_acc,
    fs_send, fs_recv, fx_send, fx_recv,
    ag_send, ag_recv, az_send, az_recv, as_send, as_recv,
    rs_send, rs_recv, rz_send, rz_recv, rb_send, rb_recv,
):
    Q, F, R, W, H, D = s.chips, s.fsdp, s.rows, s.width, s.hidden, s.model
    T = s.tokens
    HL = H // F
    half = Q * 2 * PAD
    e, z = lax.axis_index("expert"), lax.axis_index("fsdp")
    q, zh, c = e // 4, (e // 2) % 2, e % 2

    def place(q_, zh_, c_):
        return (q_ * 4 + zh_ * 2 + c_, z)

    far, twin = place(q, 1 - zh, c), place(q, zh, 1 - c)

    def chip(i):
        return lax.rem(q + i, Q)

    def line(i):
        return lax.rem(z + i, F)

    def copy(src, dst, send, recv, device):
        return pltpu.make_async_remote_copy(
            src_ref=src, dst_ref=dst, send_sem=send, recv_sem=recv, device_id=device, device_id_type=MESH
        )

    def each(count, fn):
        lax.fori_loop(1, count, lambda i, t: (fn(i), t)[1], 0)

    pending = []

    barrier = pltpu.get_barrier_semaphore()

    def greet(device):
        pl.semaphore_signal(barrier, inc=1, device_id=device, device_id_type=MESH)

    each(F, lambda i: greet((e, line(i))))
    each(Q, lambda i: greet(place(chip(i), zh, c)))
    greet(far)
    greet(twin)
    pl.semaphore_wait(barrier, F + Q)

    def ag_hop(k, a, wave, i):
        src = a.at[c, q, zh if wave == 0 else 1 - zh]
        return copy(src, src, ag_send.at[k, wave, i], ag_recv.at[k, wave, i], place(chip(i), zh, c))

    def ag_far(k, a):
        src = a.at[c, q, zh]
        return copy(src, src, az_send.at[k], az_recv.at[k], far)

    def ag_twin(k, a):
        return copy(a.at[c], a.at[c], as_send.at[k], as_recv.at[k], twin)

    def ag_start(k, a):
        ag_far(k, a).start()
        each(Q, lambda i: ag_hop(k, a, 0, i).start())

    def ag_forward(k, a):
        ag_far(k, a).wait_recv()
        each(Q, lambda i: ag_hop(k, a, 1, i).start())

    def ag_join(k, a):
        each(Q, lambda i: ag_hop(k, a, 0, i).wait_recv())
        each(Q, lambda i: ag_hop(k, a, 1, i).wait_recv())
        ag_twin(k, a).start()

    def ag_finish(k, a):
        ag_twin(k, a).wait_recv()

        def drain():
            ag_far(k, a).wait_send()
            each(Q, lambda i: ag_hop(k, a, 0, i).wait_send())
            each(Q, lambda i: ag_hop(k, a, 1, i).wait_send())
            ag_twin(k, a).wait_send()

        pending.append(drain)

    def fs_hop(k, i):
        return copy(pbuf.at[k, line(i)], rbuf.at[k, i], fs_send.at[k, i], fs_recv.at[k, i], (e, line(i)))

    def fs_ext(k, i):
        return copy(ebuf.at[k, 0], ebuf.at[k, i], fx_send.at[k, i], fx_recv.at[k, i], (e, line(i)))

    def fs_fill(k, value):
        for j in range(F):
            pbuf[k, j] = value[:, j * HL : (j + 1) * HL].astype(BF)

    def fs_start(k):
        each(F, lambda i: fs_hop(k, i).start())
        pending.append(lambda: each(F, lambda i: fs_hop(k, i).wait_send()))

    def fs_sum(k):
        total = pbuf[k, z].astype(F32)
        for i in range(1, F):
            fs_hop(k, i).wait_recv()
            total = total + rbuf[k, i].astype(F32)
        return total

    def ext_start(k, value):
        ebuf[k, 0] = value
        each(F, lambda i: fs_ext(k, i).start())
        pending.append(lambda: each(F, lambda i: fs_ext(k, i).wait_send()))

    def ext_sum(k):
        total = ebuf[k, 0]
        for i in range(1, F):
            fs_ext(k, i).wait_recv()
            total = total + ebuf[k, i]
        return total

    def fg_hop(k, i):
        return copy(full.at[k, z], full.at[k, z], fs_send.at[4 + k, i], fs_recv.at[4 + k, i], (e, line(i)))

    def fg_start(k, value):
        full[k, z] = value
        each(F, lambda i: fg_hop(k, i).start())
        pending.append(lambda: each(F, lambda i: fg_hop(k, i).wait_send()))

    def fg_wait(k):
        each(F, lambda i: fg_hop(k, i).wait_recv())

    def fg_value(k):
        return jnp.concatenate([full[k, j] for j in range(F)], axis=1)

    def rs_twin(k):
        return copy(sb.at[k], sib.at[k], rb_send.at[k], rb_recv.at[k], twin)

    def rs_hop(k, i):
        return copy(tb.at[k, chip(i)], rb.at[k, i], rs_send.at[k, i], rs_recv.at[k, i], place(chip(i), zh, c))

    def rs_far(k):
        return copy(ub.at[k], zb.at[k], rz_send.at[k], rz_recv.at[k], far)

    def rs_start(k, loop, value):
        theirs = dot(ps[loop, 1 - c], value, 1, 0)
        sb[k] = theirs.astype(BF).reshape(Q, 2, PAD, W)
        rs_twin(k).start()
        tb[k] = dot(ps[loop, c], value, 1, 0).astype(BF).reshape(Q, 2, PAD, W)

    def rs_spread(k):
        rs_twin(k).wait_recv()
        tb[k] = (tb[k].astype(F32) + sib[k].astype(F32)).astype(BF)
        each(Q, lambda i: rs_hop(k, i).start())

    def rs_gather(k):
        total = tb[k, q].astype(F32)
        for i in range(1, Q):
            rs_hop(k, i).wait_recv()
            total = total + rb[k, i].astype(F32)
        uf[k] = total
        ub[k] = uf[k, 1 - zh].astype(BF)
        rs_far(k).start()

    def rs_total(k):
        rs_far(k).wait_recv()

        def drain():
            rs_twin(k).wait_send()
            each(Q, lambda i: rs_hop(k, i).wait_send())
            rs_far(k).wait_send()

        pending.append(drain)
        return (uf[k, zh] + zb[k].astype(F32))[0:T]

    lanes = iota((T, 2 * MARKS), 1)
    named = jnp.zeros((T, 2 * MARKS), jnp.bool_)
    r0, r1 = routes_ref[0], routes_ref[1]
    for k in range(s.top):
        chosen = jnp.where(lanes < MARKS, r0[:, k : k + 1], r1[:, k : k + 1] + MARKS)
        named = named | (chosen == lanes)
    marks = jnp.where(named, 1.0, 0.0)
    earlier = jnp.zeros((T, 2 * MARKS), F32)
    t_of = iota((T, 2 * MARKS), 0)
    for t in range(T - 1):
        earlier = earlier + jnp.where(t_of > t, marks[t : t + 1], 0.0)
    ax[c, q, zh] = jnp.zeros((PAD, W + 2 * MARKS), BF)
    ax[c, q, zh, 0:T, 0:W] = x_ref[...]
    ax[c, q, zh, 0:T, W:] = (marks * (1.0 + earlier)).astype(BF)
    ag_start(0, ax)
    ac[c, q, zh] = jnp.zeros((PAD, W), BF)
    ac[c, q, zh, 0:T] = cot_ref[...]
    a1[c, q, zh] = jnp.zeros((PAD, W), BF)
    a2[c, q, zh] = jnp.zeros((PAD, W), BF)
    gain = gain_ref[...]
    sel_pick = jnp.where(iota((8, s.experts), 1) == e, 1.0, 0.0).astype(BF)
    sel_row = dot(sel_pick, sel_ref[...], 1, 1)

    ag_forward(0, ax)
    ag_start(1, ac)
    ag_join(0, ax)
    ag_finish(0, ax)

    def build(loop):
        n = 2 * half
        table = ax[:, :, :, :, W:].reshape(n, 2 * MARKS)
        mine = iota((8, 2 * MARKS), 1) == e + loop * MARKS
        wide = dot(jnp.where(mine, 1.0, 0.0).astype(BF), table, 1, 1)[0:1]
        wide_i = wide.astype(jnp.int32)
        row = jnp.where(wide_i > 0, 3 * (iota((1, n), 1) // PAD) + wide_i - 1, -1)
        pg[loop] = jnp.where(iota((R, n), 0) == row, 1.0, 0.0).astype(BF)
        picked = iota((n, 2 * MARKS), 1) == e + loop * MARKS
        tall = jnp.sum(jnp.where(picked, table.astype(F32), 0.0), axis=1, keepdims=True).astype(jnp.int32)
        place_ = jnp.where(tall > 0, 3 * (iota((n, 1), 0) // PAD) + tall - 1, -1)
        ps[loop] = (
            jnp.where(iota((n, R), 1) == place_, 1.0, 0.0).astype(BF).reshape(2, half, R)
        )

    def gathered(a):
        return a[:, :, :, :, 0:W].reshape(2 * half, W)

    def forward_in(loop, a):
        xr = dot(pg[loop], gathered(a), 1, 0)
        rows[loop] = xr.astype(BF)
        y = xr * gain
        yb = y.astype(BF)
        fs_fill(loop, dot(yb, up_ref[...], 1, 0))
        fs_start(loop)
        squares = dot(jnp.ones((8, W), F32), xr * xr, 1, 1, HIGHEST)
        logits = dot(sel_row, y, 1, 1, HIGHEST)
        ext_start(loop, two_rows(squares, logits))

    def forward_mid(loop):
        ext = ext_sum(loop)
        inv_l = lax.rsqrt(ext[0:1] / D + EPSILON)
        logit_l = ext[1:2] * inv_l
        gate_l = jax.nn.sigmoid(logit_l)
        inv, gate = column(inv_l), column(gate_l)
        pre = fs_sum(loop) * inv
        sig = jax.nn.sigmoid(pre)
        hid = (pre * sig).astype(BF)
        pre_k[loop] = pre
        slope_k[loop] = sig * (1.0 + pre * (1.0 - sig))
        hid_k[loop] = hid
        return SimpleNamespace(inv=inv, gate=gate, gate_l=gate_l, logit_l=logit_l, hid=hid)

    def forward_out(loop, st, k):
        out = dot(fg_value(loop), down_ref[...], 1, 0).astype(BF).astype(F32)
        rs_start(k, loop, (st.gate * out).astype(BF))

    def backward_in(loop, a):
        gr = dot(pg[loop], gathered(a), 1, 0).astype(BF)
        grads[loop] = gr
        fs_fill(2 + loop, dot(gr, down_ref[...], 1, 1))

    def backward_mid(loop, st):
        dh = dh_k[loop]
        hg = (st.gate * dh * slope_k[loop]).astype(BF)
        fg_start(2 + loop, hg)
        ones = jnp.ones((8, HL), F32)
        gg = dot(ones, hid_k[loop].astype(F32) * dh, 1, 1, HIGHEST)
        inner = dot(ones, hg.astype(F32) * pre_k[loop], 1, 1, HIGHEST)
        ext_start(2 + loop, two_rows(gg, inner))

    def backward_out(loop, st, k):
        ext = ext_sum(2 + loop)
        lgr_l = ext[0:1] * st.gate_l * (1.0 - st.gate_l)
        inner_l = ext[1:2] + lgr_l * st.logit_l
        lgr, inner = column(lgr_l), column(inner_l)
        fg_wait(2 + loop)
        bg = dot(fg_value(2 + loop), up_ref[...], 1, 1).astype(BF).astype(F32)
        xr = rows[loop].astype(F32)
        ng = bg + lgr * sel_row[0:1]
        contribution = st.inv * gain * ng - (st.inv * st.inv / D) * inner * xr
        rs_start(k, loop, contribution.astype(BF))
        return lgr_l

    def normed(loop, st):
        return (rows[loop].astype(F32) * st.inv * gain).astype(BF)

    def d_sent(loop, st):
        return (grads[loop].astype(F32) * st.gate).astype(BF)

    build(0)
    forward_in(0, ax)
    build(1)
    ag_forward(1, ac)
    ag_join(1, ac)
    ag_finish(1, ac)
    backward_in(1, ac)
    st0 = forward_mid(0)
    fg_start(0, st0.hid)
    fs_start(3)
    fg_wait(0)
    forward_out(0, st0, 0)
    rs_spread(0)
    dh_k[1] = fs_sum(3)
    rs_gather(0)
    x1 = (x_ref[...].astype(F32) + rs_total(0)).astype(BF)
    a1[c, q, zh, 0:T] = x1
    ag_start(2, a1)
    ag_forward(2, a1)
    ag_join(2, a1)
    ag_finish(2, a1)
    forward_in(1, a1)
    st1 = forward_mid(1)
    backward_mid(1, st1)
    fg_start(1, st1.hid)
    lgr1_l = backward_out(1, st1, 2)
    rs_spread(2)
    n1 = normed(1, st1)
    up_acc[...] = dot(n1, fg_value(3), 0, 0)
    rs_gather(2)
    fg_wait(1)
    down_acc[...] = dot(fg_value(1), d_sent(1, st1), 0, 0)
    sel_acc = dot(jnp.broadcast_to(lgr1_l, (8, R)), n1.astype(F32), 1, 0, HIGHEST)
    g1 = (cot_ref[...].astype(F32) + rs_total(2)).astype(BF)
    a2[c, q, zh, 0:T] = g1
    ag_start(3, a2)
    forward_out(1, st1, 1)
    ag_forward(3, a2)
    ag_join(3, a2)
    ag_finish(3, a2)
    backward_in(0, a2)
    fs_start(2)
    rs_spread(1)
    ddown_ref[...] = (down_acc[...] + dot(fg_value(0), d_sent(0, st0), 0, 0)).astype(BF)
    dh_k[0] = fs_sum(2)
    backward_mid(0, st0)
    rs_gather(1)
    lgr0_l = backward_out(0, st0, 3)
    n0 = normed(0, st0)
    sel_acc = sel_acc + dot(jnp.broadcast_to(lgr0_l, (8, R)), n0.astype(F32), 1, 0, HIGHEST)
    tile = jnp.zeros((8, 128), F32)
    for i in range(W // 128):
        tile = jnp.where(iota((8, 128), 0) == i, sel_acc[:, i * 128 : (i + 1) * 128], tile)
    asel[c, q, zh] = tile
    ag_start(4, asel)
    rs_spread(3)
    up0 = dot(n0, fg_value(2), 0, 0)
    dup_ref[...] = (up_acc[...] + up0).astype(BF)
    ag_forward(4, asel)
    rs_gather(3)
    mixed_ref[...] = (a1[c, q, zh, 0:T].astype(F32) + rs_total(1)).astype(BF)
    ag_join(4, asel)
    ag_finish(4, asel)
    dtok_ref[...] = (a2[c, q, zh, 0:T].astype(F32) + rs_total(3)).astype(BF)
    for i in range(W // 128):
        stack = asel[:, :, :, i, :].reshape(2, 2 * Q, 128)
        both = jnp.stack([stack[0], stack[1]], axis=1).reshape(4 * Q, 128)
        dsel_ref[i * 128 : (i + 1) * 128, :] = both.T
    for drain in pending:
        drain()


def shards(s, tokens, gain, w_sel, w_up, w_down, routes, cotangent):
    Q, F, R, W, H = s.chips, s.fsdp, s.rows, s.width, s.hidden
    HL = H // F
    VM, DMA = pltpu.VMEM, pltpu.SemaphoreType.DMA
    half = Q * 2 * PAD
    gather = lambda w, t=BF, r=PAD: VM((2, Q, 2, r, w), t)
    scratch = [
        gather(W + 2 * MARKS), gather(W), gather(W), gather(W), gather(128, F32, 8),
        VM((4, F, R, HL), BF), VM((4, F, R, HL), BF), VM((4, F, R, HL), BF),
        VM((4, F, 8, R), F32), VM((8, 128), F32),
        VM((4, Q, 2, PAD, W), BF), VM((4, Q, 2, PAD, W), BF), VM((4, Q, 2, PAD, W), BF), VM((4, Q, 2, PAD, W), BF),
        VM((4, 2, PAD, W), F32), VM((4, PAD, W), BF), VM((4, PAD, W), BF),
        VM((2, R, 2 * half), BF), VM((2, 2, half, R), BF),
        VM((2, R, HL), F32), VM((2, R, HL), F32), VM((2, R, HL), BF), VM((2, R, HL), F32),
        VM((2, R, W), BF), VM((2, R, W), BF), VM((W, H), F32), VM((H, W), F32),
        DMA((8, F)), DMA((8, F)), DMA((4, F)), DMA((4, F)),
        DMA((5, 2, Q)), DMA((5, 2, Q)), DMA((5,)), DMA((5,)), DMA((5,)), DMA((5,)),
        DMA((4, Q)), DMA((4, Q)), DMA((4,)), DMA((4,)), DMA((4,)), DMA((4,)),
    ]
    T = tokens.shape[0]
    out = pl.pallas_call(
        functools.partial(kernel, s),
        out_shape=(
            jax.ShapeDtypeStruct((T, W), BF),
            jax.ShapeDtypeStruct((T, W), BF),
            jax.ShapeDtypeStruct((W, H), BF),
            jax.ShapeDtypeStruct((H, W), BF),
            jax.ShapeDtypeStruct((W, s.experts), F32),
        ),
        in_specs=[pl.BlockSpec(memory_space=pltpu.VMEM)] * 7,
        out_specs=[pl.BlockSpec(memory_space=pltpu.VMEM)] * 5,
        scratch_shapes=scratch,
        compiler_params=pltpu.CompilerParams(
            collective_id=0, has_side_effects=True, vmem_limit_bytes=60 * 1024 * 1024
        ),
        cost_estimate=pl.CostEstimate(flops=6 * 10**9, bytes_accessed=5 * 2**20, transcendentals=10**5),
    )(tokens, cotangent, gain.reshape(1, W), w_sel, w_up[0], w_down[0], routes)
    mixed, d_tokens, d_up, d_down, d_sel = out
    return mixed, d_tokens, d_up[None], d_down[None], d_sel


def solution(mesh):
    n_expert, fsdp = mesh.shape["expert"], mesh.shape["fsdp"]

    def whole(tokens, gain, w_sel, w_up, w_down, routes, cotangent):
        s = SimpleNamespace(
            chips=n_expert // 4,
            fsdp=fsdp,
            tokens=tokens.shape[0] // n_expert,
            rows=n_expert * 3,
            width=tokens.shape[1] // fsdp,
            model=tokens.shape[1],
            hidden=w_up.shape[2],
            experts=w_sel.shape[1],
            top=routes.shape[2],
        )
        return jax.shard_map(
            functools.partial(shards, s),
            mesh=mesh,
            in_specs=(
                P("expert", "fsdp"),
                P("fsdp"),
                P("fsdp", None),
                P("expert", "fsdp", None),
                P("expert", None, "fsdp"),
                P(None, "expert", None),
                P("expert", "fsdp"),
            ),
            out_specs=(
                P("expert", "fsdp"),
                P("expert", "fsdp"),
                P("expert", "fsdp", None),
                P("expert", None, "fsdp"),
                P("fsdp", None),
            ),
            check_vma=False,
        )(tokens, gain, w_sel, w_up, w_down, routes, cotangent)

    return whole
```

time: 1920 us -> 283 us (0.15)
  waiting for transfers between devices: 1450 us -> 0 us
  blocking collectives: 333 us -> 0 us
  Pallas kernels: 0 us -> 271 us
  starting transfers between devices: 77.4 us -> 0 us
  matrix products: 26.3 us -> 0 us
    psum x5 -> x0, waiting for transfers between devices: 1380 us -> none  [the longest x1 965 us: shards(): select_grad = lax.psum(select_total, 'expert')]
    pallas_call x0 -> x1, Pallas kernels: none -> 271 us  [shards(): pl.pallas_call(functools.partial(kernel, s), out_shape=(jax.ShapeDtypeStr...]
    psum x7 -> x0, blocking collectives: 218 us -> none  [the longest x2 80.2 us: shards(): lax.psum(jnp.dot(normed, w_sel, preferred_element_type=jnp.float32), 'fsdp')]
    all_to_all x3 -> x0, blocking collectives: 115 us -> none  [send_rows(): lax.all_to_all(packed.reshape(experts, capacity, local_width), 'expert',...]
    all_to_all x5 -> x0, starting transfers between devices: 77.2 us -> none  [the longest x4 63.6 us: return_rows(): lax.all_to_all(expert_rows.reshape(experts, capacity, local_width), 'expe...]
    all_to_all x5 -> x0, waiting for transfers between devices: 67.4 us -> none  [the longest x4 49 us: return_rows(): lax.all_to_all(expert_rows.reshape(experts, capacity, local_width), 'expe...]
    dot_general x26 -> x0, matrix products: 26.3 us -> none  [the longest x2 6.44 us: shards(): jnp.einsum('hr,rd->hd', hidden, grad_rows, preferred_element_type=jnp.flo...]
  transfers between devices with their start and end apart: 10 -> 0, of which waited for: 9 -> 0; matrix products, arithmetic and copies ran while one was open for 1% -> 0% of each run, Pallas kernels for 0% -> 0%
where the time goes in v1:
time: 283 us; the launch traced here: 281 us
  Pallas kernels  271 us (96%)
  local copies, waits for them, and re-layouts  9.37 us (3%)
    pallas_call x1, Pallas kernels, shards(): pl.pallas_call(functools.partial(kernel, s), out_shape=(jax.ShapeDtypeStr...  271 us
    unnamed x13, local copies, waits for them, and re-layouts  9.37 us

profile of v1, /device:TPU:1, one launch (start us, length us, event | category | flops | bytes accessed | tf_op | source)
XLA Modules:
  0.0 281.2 jit_solution(2379023679349710804)
XLA Ops:
  0.6 1.4 copy.13.routes_ref
  2.0 1.6 copy.12.sel_ref
  3.6 271.2 %shard_map.110 = (bf16[12,512]{1,0:T(8,128)(2,1)}, bf16[12,512]{1,0:T(8,128)(2,1)}, bf16[512,1024]{1,0:T(8,128)(2,1)}, bf16[1024,512]{1,0:T(8,128)(2,1)}, f32[512,64]{1,0:T(8,128)}) custom-call(bf16[12,512]{1,0:T(8,128)(2,1)} %x_ref.1, bf16[12,512]{1,0:T(8,128)(2,1)} %cot_ref.1, f32[1,512]{1,0:T(1,128)} %bitcast.9, bf16[512,64]{1,0:T(8,128)(2,1)} %copy.12.sel_ref, ...), custom_call_target="tpu_custom_call" | custom-call | flops 6000000000 | bytes 5242880 | tf_op jit(solution)/shard_map/pallas_call | solution.py:411
  274.8 0.0 copy-start.2
  274.8 1.7 copy.14
  276.5 0.0 copy-done.2
  276.5 0.0 copy-start.1
  276.5 0.6 copy.19
  277.1 0.1 copy-done.1
  277.3 0.6 copy.20
  277.9 0.0 copy-start
  277.9 2.4 copy.21
  280.2 0.0 copy-done
  280.2 1.0 copy.22
Async XLA Ops:
  274.8 1.7 copy-start.2
  276.5 0.7 copy-start.1
  277.9 2.4 copy-start

commit v2 on v1

--- a/solution.py
+++ b/solution.py
@@ -14,6 +14,7 @@
 BF, F32 = jnp.bfloat16, jnp.float32
 PAD = 16
 MARKS = 64
+CHUNKS = 2
 
 
 def iota(shape, dim):
@@ -40,10 +41,10 @@
     x_ref, cot_ref, gain_ref, sel_ref, up_ref, down_ref, routes_ref,
     mixed_ref, dtok_ref, dup_ref, ddown_ref, dsel_ref,
     ax, ac, a1, a2, asel,
-    pbuf, rbuf, full, ebuf, gbuf,
-    sb, sib, tb, rb, uf, ub, zb,
+    pbuf, nbuf, qbuf, rbuf, full, ebuf,
+    sb, sib, tb, rb, ub, zb,
     pg, ps, pre_k, slope_k, hid_k, dh_k, rows, grads, up_acc, down_acc,
-    fs_send, fs_recv, fx_send, fx_recv,
+    fn_send, fn_recv, fs_send, fs_recv, fx_send, fx_recv,
     ag_send, ag_recv, az_send, az_recv, as_send, as_recv,
     rs_send, rs_recv, rz_send, rz_recv, rb_send, rb_recv,
 ):
@@ -57,6 +58,13 @@
     def place(q_, zh_, c_):
         return (q_ * 4 + zh_ * 2 + c_, z)
 
+    RC = R // CHUNKS
+    par, m = z % 2, z // 2
+    near = (e, z + 1 - 2 * par)
+
+    def quad(i):
+        return lax.rem(m + i, F // 2)
+
     far, twin = place(q, 1 - zh, c), place(q, zh, 1 - c)
 
     def chip(i):
@@ -74,6 +82,11 @@
         lax.fori_loop(1, count, lambda i, t: (fn(i), t)[1], 0)
 
     pending = []
+
+    def settle():
+        for drain in pending:
+            drain()
+        pending.clear()
 
     barrier = pltpu.get_barrier_semaphore()
 
@@ -94,8 +107,17 @@
         src = a.at[c, q, zh]
         return copy(src, src, az_send.at[k], az_recv.at[k], far)
 
-    def ag_twin(k, a):
-        return copy(a.at[c], a.at[c], as_send.at[k], as_recv.at[k], twin)
+    def ag_twin(k, a, i):
+        src = a.at[c, lax.rem(q + Q - i, Q)]
+        return copy(src, src, as_send.at[k, i], as_recv.at[k, i], twin)
+
+    def ag_twin_wait(k, a):
+        ag_twin(k, a, 0).wait_recv()
+        each(Q, lambda i: ag_twin(k, a, i).wait_recv())
+
+    def ag_twin_drain(k, a):
+        ag_twin(k, a, 0).wait_send()
+        each(Q, lambda i: ag_twin(k, a, i).wait_send())
 
     def ag_start(k, a):
         ag_far(k, a).start()
@@ -104,42 +126,87 @@
     def ag_forward(k, a):
         ag_far(k, a).wait_recv()
         each(Q, lambda i: ag_hop(k, a, 1, i).start())
+        ag_twin(k, a, 0).start()
+
+    def ag_pair_hop(k, a, i):
+        src = a.at[c, q]
+        return copy(src, src, ag_send.at[k, 0, i], ag_recv.at[k, 0, i], place(chip(i), zh, c))
+
+    def ag_pair(k, a):
+        each(Q, lambda i: ag_pair_hop(k, a, i).start())
+        ag_twin(k, a, 0).start()
+
+    def ag_pair_join(k, a):
+        def pass_on(i):
+            ag_pair_hop(k, a, i).wait_recv()
+            ag_twin(k, a, i).start()
+
+        each(Q, pass_on)
+
+    def ag_pair_finish(k, a):
+        ag_twin_wait(k, a)
+
+        def drain():
+            each(Q, lambda i: ag_pair_hop(k, a, i).wait_send())
+            ag_twin_drain(k, a)
+
+        pending.append(drain)
 
     def ag_join(k, a):
-        each(Q, lambda i: ag_hop(k, a, 0, i).wait_recv())
-        each(Q, lambda i: ag_hop(k, a, 1, i).wait_recv())
-        ag_twin(k, a).start()
+        def pass_on(i):
+            ag_hop(k, a, 0, i).wait_recv()
+            ag_hop(k, a, 1, i).wait_recv()
+            ag_twin(k, a, i).start()
+
+        each(Q, pass_on)
 
     def ag_finish(k, a):
-        ag_twin(k, a).wait_recv()
+        ag_twin_wait(k, a)
 
         def drain():
             ag_far(k, a).wait_send()
             each(Q, lambda i: ag_hop(k, a, 0, i).wait_send())
             each(Q, lambda i: ag_hop(k, a, 1, i).wait_send())
-            ag_twin(k, a).wait_send()
+            ag_twin_drain(k, a)
 
         pending.append(drain)
 
-    def fs_hop(k, i):
-        return copy(pbuf.at[k, line(i)], rbuf.at[k, i], fs_send.at[k, i], fs_recv.at[k, i], (e, line(i)))
+    def fs_near(k, p):
+        src = pbuf.at[k, p, 1 - par]
+        return copy(src, nbuf.at[k, p], fn_send.at[k, p], fn_recv.at[k, p], near)
+
+    def fs_hop(k, p, i):
+        src, dst = qbuf.at[k, p, quad(i)], rbuf.at[k, p, i]
+        return copy(src, dst, fs_send.at[k, p, i], fs_recv.at[k, p, i], (e, 2 * quad(i) + par))
 
     def fs_ext(k, i):
         return copy(ebuf.at[k, 0], ebuf.at[k, i], fx_send.at[k, i], fx_recv.at[k, i], (e, line(i)))
 
-    def fs_fill(k, value):
-        for j in range(F):
-            pbuf[k, j] = value[:, j * HL : (j + 1) * HL].astype(BF)
-
-    def fs_start(k):
-        each(F, lambda i: fs_hop(k, i).start())
-        pending.append(lambda: each(F, lambda i: fs_hop(k, i).wait_send()))
-
-    def fs_sum(k):
-        total = pbuf[k, z].astype(F32)
-        for i in range(1, F):
-            fs_hop(k, i).wait_recv()
-            total = total + rbuf[k, i].astype(F32)
+    def fs_fill(k, part_of):
+        for p in range(CHUNKS):
+            value = part_of(slice(p * RC, (p + 1) * RC))
+            for j in range(F):
+                pbuf[k, p, j % 2, j // 2] = value[:, j * HL : (j + 1) * HL].astype(BF)
+            fs_near(k, p).start()
+
+    def fs_spread(k):
+        for p in range(CHUNKS):
+            fs_near(k, p).wait_recv()
+            qbuf[k, p] = (pbuf[k, p, par].astype(F32) + nbuf[k, p].astype(F32)).astype(BF)
+            each(F // 2, lambda i: fs_hop(k, p, i).start())
+
+        def drain():
+            for p in range(CHUNKS):
+                fs_near(k, p).wait_send()
+                each(F // 2, lambda i: fs_hop(k, p, i).wait_send())
+
+        pending.append(drain)
+
+    def fs_sum(k, p):
+        total = qbuf[k, p, m].astype(F32)
+        for i in range(1, F // 2):
+            fs_hop(k, p, i).wait_recv()
+            total = total + rbuf[k, p, i].astype(F32)
         return total
 
     def ext_start(k, value):
@@ -154,19 +221,39 @@
             total = total + ebuf[k, i]
         return total
 
-    def fg_hop(k, i):
-        return copy(full.at[k, z], full.at[k, z], fs_send.at[4 + k, i], fs_recv.at[4 + k, i], (e, line(i)))
-
-    def fg_start(k, value):
-        full[k, z] = value
-        each(F, lambda i: fg_hop(k, i).start())
-        pending.append(lambda: each(F, lambda i: fg_hop(k, i).wait_send()))
+    def fg_hop(k, p, i):
+        src = full.at[k, p, par, m]
+        return copy(src, src, fs_send.at[4 + k, p, i], fs_recv.at[4 + k, p, i], (e, 2 * quad(i) + par))
+
+    def fg_near(k, p):
+        src = full.at[k, p, par]
+        return copy(src, src, fn_send.at[4 + k, p], fn_recv.at[4 + k, p], near)
+
+    def fg_start(k, p, value):
+        full[k, p, par, m] = value
+        each(F // 2, lambda i: fg_hop(k, p, i).start())
+
+    def fg_forward(k):
+        for p in range(CHUNKS):
+            each(F // 2, lambda i: fg_hop(k, p, i).wait_recv())
+            fg_near(k, p).start()
 
     def fg_wait(k):
-        each(F, lambda i: fg_hop(k, i).wait_recv())
+        for p in range(CHUNKS):
+            fg_near(k, p).wait_recv()
+
+        def drain():
+            for p in range(CHUNKS):
+                fg_near(k, p).wait_send()
+                each(F // 2, lambda i: fg_hop(k, p, i).wait_send())
+
+        pending.append(drain)
 
     def fg_value(k):
-        return jnp.concatenate([full[k, j] for j in range(F)], axis=1)
+        parts = [
+            jnp.concatenate([full[k, p, j % 2, j // 2] for j in range(F)], axis=1) for p in range(CHUNKS)
+        ]
+        return jnp.concatenate(parts, axis=0)
 
     def rs_twin(k):
         return copy(sb.at[k], sib.at[k], rb_send.at[k], rb_recv.at[k], twin)
@@ -175,6 +262,8 @@
         return copy(tb.at[k, chip(i)], rb.at[k, i], rs_send.at[k, i], rs_recv.at[k, i], place(chip(i), zh, c))
 
     def rs_far(k):
+        if k % 2:
+            return copy(ub.at[k, 1 - zh], zb.at[k, 1 - zh], rz_send.at[k], rz_recv.at[k], far)
         return copy(ub.at[k], zb.at[k], rz_send.at[k], rz_recv.at[k], far)
 
     def rs_start(k, loop, value):
@@ -193,8 +282,7 @@
         for i in range(1, Q):
             rs_hop(k, i).wait_recv()
             total = total + rb[k, i].astype(F32)
-        uf[k] = total
-        ub[k] = uf[k, 1 - zh].astype(BF)
+        ub[k] = total.astype(BF)
         rs_far(k).start()
 
     def rs_total(k):
@@ -206,11 +294,14 @@
             rs_far(k).wait_send()
 
         pending.append(drain)
-        return (uf[k, zh] + zb[k].astype(F32))[0:T]
+        if k % 2:
+            return (ub[k, zh].astype(F32) + zb[k, zh].astype(F32))[0:T]
+        return ub[k].astype(F32) + zb[k].astype(F32)
 
     lanes = iota((T, 2 * MARKS), 1)
     named = jnp.zeros((T, 2 * MARKS), jnp.bool_)
-    r0, r1 = routes_ref[0], routes_ref[1]
+    unit = jnp.where(iota((T, T), 0) == iota((T, T), 1), 1.0, 0.0).astype(BF)
+    r0, r1 = (dot(unit, routes_ref[i].astype(F32).astype(BF), 1, 1).astype(jnp.int32) for i in range(2))
     for k in range(s.top):
         chosen = jnp.where(lanes < MARKS, r0[:, k : k + 1], r1[:, k : k + 1] + MARKS)
         named = named | (chosen == lanes)
@@ -225,25 +316,29 @@
     ag_start(0, ax)
     ac[c, q, zh] = jnp.zeros((PAD, W), BF)
     ac[c, q, zh, 0:T] = cot_ref[...]
-    a1[c, q, zh] = jnp.zeros((PAD, W), BF)
-    a2[c, q, zh] = jnp.zeros((PAD, W), BF)
     gain = gain_ref[...]
     sel_pick = jnp.where(iota((8, s.experts), 1) == e, 1.0, 0.0).astype(BF)
-    sel_row = dot(sel_pick, sel_ref[...], 1, 1)
+    sel_row = dot(sel_pick, sel_ref[...], 1, 0)
 
     ag_forward(0, ax)
-    ag_start(1, ac)
     ag_join(0, ax)
     ag_finish(0, ax)
 
-    def build(loop):
-        n = 2 * half
-        table = ax[:, :, :, :, W:].reshape(n, 2 * MARKS)
+    n = 2 * half
+
+    def marks_table():
+        return ax[:, :, :, :, W:].reshape(n, 2 * MARKS)
+
+    def build_gather(loop):
+        table = marks_table()
         mine = iota((8, 2 * MARKS), 1) == e + loop * MARKS
         wide = dot(jnp.where(mine, 1.0, 0.0).astype(BF), table, 1, 1)[0:1]
         wide_i = wide.astype(jnp.int32)
         row = jnp.where(wide_i > 0, 3 * (iota((1, n), 1) // PAD) + wide_i - 1, -1)
         pg[loop] = jnp.where(iota((R, n), 0) == row, 1.0, 0.0).astype(BF)
+
+    def build_scatter(loop):
+        table = marks_table()
         picked = iota((n, 2 * MARKS), 1) == e + loop * MARKS
         tall = jnp.sum(jnp.where(picked, table.astype(F32), 0.0), axis=1, keepdims=True).astype(jnp.int32)
         place_ = jnp.where(tall > 0, 3 * (iota((n, 1), 0) // PAD) + tall - 1, -1)
@@ -259,8 +354,7 @@
         rows[loop] = xr.astype(BF)
         y = xr * gain
         yb = y.astype(BF)
-        fs_fill(loop, dot(yb, up_ref[...], 1, 0))
-        fs_start(loop)
+        fs_fill(loop, lambda part: dot(yb[part], up_ref[...], 1, 0))
         squares = dot(jnp.ones((8, W), F32), xr * xr, 1, 1, HIGHEST)
         logits = dot(sel_row, y, 1, 1, HIGHEST)
         ext_start(loop, two_rows(squares, logits))
@@ -271,13 +365,21 @@
         logit_l = ext[1:2] * inv_l
         gate_l = jax.nn.sigmoid(logit_l)
         inv, gate = column(inv_l), column(gate_l)
-        pre = fs_sum(loop) * inv
-        sig = jax.nn.sigmoid(pre)
-        hid = (pre * sig).astype(BF)
-        pre_k[loop] = pre
-        slope_k[loop] = sig * (1.0 + pre * (1.0 - sig))
-        hid_k[loop] = hid
-        return SimpleNamespace(inv=inv, gate=gate, gate_l=gate_l, logit_l=logit_l, hid=hid)
+        st = SimpleNamespace(inv=inv, gate=gate, gate_l=gate_l, logit_l=logit_l)
+        for p in range(CHUNKS):
+            part = slice(p * RC, (p + 1) * RC)
+            pre = fs_sum(loop, p) * inv[part]
+            sig = jax.nn.sigmoid(pre)
+            hid = (pre * sig).astype(BF)
+            slope = sig * (1.0 + pre * (1.0 - sig))
+            pre_k[loop, part] = pre
+            slope_k[loop, part] = slope
+            hid_k[loop, part] = hid
+            if loop == 0:
+                fg_start(0, p, hid)
+            else:
+                fg_start(3, p, (gate[part] * dh_k[1, part] * slope).astype(BF))
+        return st
 
     def forward_out(loop, st, k):
         out = dot(fg_value(loop), down_ref[...], 1, 0).astype(BF).astype(F32)
@@ -286,12 +388,18 @@
     def backward_in(loop, a):
         gr = dot(pg[loop], gathered(a), 1, 0).astype(BF)
         grads[loop] = gr
-        fs_fill(2 + loop, dot(gr, down_ref[...], 1, 1))
+        fs_fill(2 + loop, lambda part: dot(gr[part], down_ref[...], 1, 1))
 
     def backward_mid(loop, st):
+        for p in range(CHUNKS):
+            part = slice(p * RC, (p + 1) * RC)
+            dh = fs_sum(2 + loop, p)
+            dh_k[loop, part] = dh
+            fg_start(2 + loop, p, (st.gate[part] * dh * slope_k[loop, part]).astype(BF))
+
+    def backward_ext(loop, st):
         dh = dh_k[loop]
         hg = (st.gate * dh * slope_k[loop]).astype(BF)
-        fg_start(2 + loop, hg)
         ones = jnp.ones((8, HL), F32)
         gg = dot(ones, hid_k[loop].astype(F32) * dh, 1, 1, HIGHEST)
         inner = dot(ones, hg.astype(F32) * pre_k[loop], 1, 1, HIGHEST)
@@ -316,55 +424,65 @@
     def d_sent(loop, st):
         return (grads[loop].astype(F32) * st.gate).astype(BF)
 
-    build(0)
+    build_gather(0)
     forward_in(0, ax)
-    build(1)
+    ag_start(1, ac)
+    build_scatter(0)
+    build_gather(1)
+    fs_spread(0)
+    build_scatter(1)
     ag_forward(1, ac)
+    st0 = forward_mid(0)
     ag_join(1, ac)
+    fg_forward(0)
     ag_finish(1, ac)
-    backward_in(1, ac)
-    st0 = forward_mid(0)
-    fg_start(0, st0.hid)
-    fs_start(3)
     fg_wait(0)
     forward_out(0, st0, 0)
     rs_spread(0)
-    dh_k[1] = fs_sum(3)
+    backward_in(1, ac)
     rs_gather(0)
-    x1 = (x_ref[...].astype(F32) + rs_total(0)).astype(BF)
-    a1[c, q, zh, 0:T] = x1
-    ag_start(2, a1)
-    ag_forward(2, a1)
-    ag_join(2, a1)
-    ag_finish(2, a1)
+    fs_spread(3)
+    both = ax[c, q, :, :, 0:W].astype(F32)
+    a1[c, q] = (both + rs_total(0)).astype(BF)
+    ag_pair(2, a1)
+    for p in range(CHUNKS):
+        dh_k[1, p * RC : (p + 1) * RC] = fs_sum(3, p)
+    ag_pair_join(2, a1)
+    ag_pair_finish(2, a1)
     forward_in(1, a1)
+    settle()
+    fs_spread(1)
     st1 = forward_mid(1)
-    backward_mid(1, st1)
-    fg_start(1, st1.hid)
+    backward_ext(1, st1)
+    fg_forward(3)
     lgr1_l = backward_out(1, st1, 2)
+    for p in range(CHUNKS):
+        fg_start(1, p, hid_k[1, p * RC : (p + 1) * RC])
     rs_spread(2)
     n1 = normed(1, st1)
     up_acc[...] = dot(n1, fg_value(3), 0, 0)
+    fg_forward(1)
     rs_gather(2)
+    sel_acc = dot(jnp.broadcast_to(lgr1_l, (8, R)), n1.astype(F32), 1, 0, HIGHEST)
     fg_wait(1)
     down_acc[...] = dot(fg_value(1), d_sent(1, st1), 0, 0)
-    sel_acc = dot(jnp.broadcast_to(lgr1_l, (8, R)), n1.astype(F32), 1, 0, HIGHEST)
-    g1 = (cot_ref[...].astype(F32) + rs_total(2)).astype(BF)
-    a2[c, q, zh, 0:T] = g1
-    ag_start(3, a2)
+    both = ac[c, q].astype(F32)
+    a2[c, q] = (both + rs_total(2)).astype(BF)
+    ag_pair(3, a2)
     forward_out(1, st1, 1)
-    ag_forward(3, a2)
-    ag_join(3, a2)
-    ag_finish(3, a2)
+    ag_pair_join(3, a2)
+    ag_pair_finish(3, a2)
     backward_in(0, a2)
-    fs_start(2)
+    settle()
     rs_spread(1)
+    fs_spread(2)
     ddown_ref[...] = (down_acc[...] + dot(fg_value(0), d_sent(0, st0), 0, 0)).astype(BF)
-    dh_k[0] = fs_sum(2)
+    n0 = normed(0, st0)
     backward_mid(0, st0)
+    backward_ext(0, st0)
     rs_gather(1)
+    fg_forward(2)
     lgr0_l = backward_out(0, st0, 3)
-    n0 = normed(0, st0)
     sel_acc = sel_acc + dot(jnp.broadcast_to(lgr0_l, (8, R)), n0.astype(F32), 1, 0, HIGHEST)
     tile = jnp.zeros((8, 128), F32)
     for i in range(W // 128):
@@ -372,39 +490,39 @@
     asel[c, q, zh] = tile
     ag_start(4, asel)
     rs_spread(3)
+    settle()
     up0 = dot(n0, fg_value(2), 0, 0)
     dup_ref[...] = (up_acc[...] + up0).astype(BF)
+    mixed_ref[...] = (a1[c, q, zh, 0:T].astype(F32) + rs_total(1)).astype(BF)
     ag_forward(4, asel)
     rs_gather(3)
-    mixed_ref[...] = (a1[c, q, zh, 0:T].astype(F32) + rs_total(1)).astype(BF)
     ag_join(4, asel)
     ag_finish(4, asel)
-    dtok_ref[...] = (a2[c, q, zh, 0:T].astype(F32) + rs_total(3)).astype(BF)
     for i in range(W // 128):
         stack = asel[:, :, :, i, :].reshape(2, 2 * Q, 128)
-        both = jnp.stack([stack[0], stack[1]], axis=1).reshape(4 * Q, 128)
-        dsel_ref[i * 128 : (i + 1) * 128, :] = both.T
-    for drain in pending:
-        drain()
+        dsel_ref[:, i * 128 : (i + 1) * 128] = jnp.stack([stack[0], stack[1]], axis=1).reshape(4 * Q, 128)
+    dtok_ref[...] = (a2[c, q, zh, 0:T].astype(F32) + rs_total(3)).astype(BF)
+    settle()
 
 
 def shards(s, tokens, gain, w_sel, w_up, w_down, routes, cotangent):
     Q, F, R, W, H = s.chips, s.fsdp, s.rows, s.width, s.hidden
-    HL = H // F
+    HL, NC = H // F, CHUNKS
+    RC = R // NC
     VM, DMA = pltpu.VMEM, pltpu.SemaphoreType.DMA
     half = Q * 2 * PAD
     gather = lambda w, t=BF, r=PAD: VM((2, Q, 2, r, w), t)
     scratch = [
         gather(W + 2 * MARKS), gather(W), gather(W), gather(W), gather(128, F32, 8),
-        VM((4, F, R, HL), BF), VM((4, F, R, HL), BF), VM((4, F, R, HL), BF),
-        VM((4, F, 8, R), F32), VM((8, 128), F32),
+        VM((4, NC, 2, F // 2, RC, HL), BF), VM((4, NC, F // 2, RC, HL), BF), VM((4, NC, F // 2, RC, HL), BF),
+        VM((4, NC, F // 2, RC, HL), BF), VM((4, NC, 2, F // 2, RC, HL), BF), VM((4, F, 8, R), F32),
         VM((4, Q, 2, PAD, W), BF), VM((4, Q, 2, PAD, W), BF), VM((4, Q, 2, PAD, W), BF), VM((4, Q, 2, PAD, W), BF),
-        VM((4, 2, PAD, W), F32), VM((4, PAD, W), BF), VM((4, PAD, W), BF),
+        VM((4, 2, PAD, W), BF), VM((4, 2, PAD, W), BF),
         VM((2, R, 2 * half), BF), VM((2, 2, half, R), BF),
         VM((2, R, HL), F32), VM((2, R, HL), F32), VM((2, R, HL), BF), VM((2, R, HL), F32),
         VM((2, R, W), BF), VM((2, R, W), BF), VM((W, H), F32), VM((H, W), F32),
-        DMA((8, F)), DMA((8, F)), DMA((4, F)), DMA((4, F)),
-        DMA((5, 2, Q)), DMA((5, 2, Q)), DMA((5,)), DMA((5,)), DMA((5,)), DMA((5,)),
+        DMA((8, NC)), DMA((8, NC)), DMA((8, NC, F // 2)), DMA((8, NC, F // 2)), DMA((4, F)), DMA((4, F)),
+        DMA((5, 2, Q)), DMA((5, 2, Q)), DMA((5,)), DMA((5,)), DMA((5, Q)), DMA((5, Q)),
         DMA((4, Q)), DMA((4, Q)), DMA((4,)), DMA((4,)), DMA((4,)), DMA((4,)),
     ]
     T = tokens.shape[0]
@@ -415,7 +533,7 @@
             jax.ShapeDtypeStruct((T, W), BF),
             jax.ShapeDtypeStruct((W, H), BF),
             jax.ShapeDtypeStruct((H, W), BF),
-            jax.ShapeDtypeStruct((W, s.experts), F32),
+            jax.ShapeDtypeStruct((s.experts, W), F32),
         ),
         in_specs=[pl.BlockSpec(memory_space=pltpu.VMEM)] * 7,
         out_specs=[pl.BlockSpec(memory_space=pltpu.VMEM)] * 5,
@@ -424,9 +542,9 @@
             collective_id=0, has_side_effects=True, vmem_limit_bytes=60 * 1024 * 1024
         ),
         cost_estimate=pl.CostEstimate(flops=6 * 10**9, bytes_accessed=5 * 2**20, transcendentals=10**5),
-    )(tokens, cotangent, gain.reshape(1, W), w_sel, w_up[0], w_down[0], routes)
+    )(tokens, cotangent, gain.reshape(1, W), w_sel.T, w_up[0], w_down[0], routes.swapaxes(1, 2))
     mixed, d_tokens, d_up, d_down, d_sel = out
-    return mixed, d_tokens, d_up[None], d_down[None], d_sel
+    return mixed, d_tokens, d_up[None], d_down[None], d_sel.T
 
 
 def solution(mesh):

time: 283 us -> 233 us (0.82)
  Pallas kernels: 271 us -> 224 us
  local copies, waits for them, and re-layouts: 9.37 us -> 5.97 us
    pallas_call x1, Pallas kernels: 271 us -> 224 us  [shards(): pl.pallas_call(functools.partial(kernel, s), out_shape=(jax.ShapeDtypeStr...]
    unnamed x13 -> x11, local copies, waits for them, and re-layouts: 9.37 us -> 5.97 us
where the time goes in v2:
time: 233 us; the launch traced here: 231 us
  Pallas kernels  224 us (96%)
  local copies, waits for them, and re-layouts  5.97 us (3%)
    pallas_call x1, Pallas kernels, shards(): pl.pallas_call(functools.partial(kernel, s), out_shape=(jax.ShapeDtypeStr...  224 us
    unnamed x11, local copies, waits for them, and re-layouts  5.97 us

profile of v2, /device:TPU:1, one launch (start us, length us, event | category | flops | bytes accessed | tf_op | source)
XLA Modules:
  0.0 231.0 jit_solution(3191704805540139360)
XLA Ops:
  0.6 224.4 %shard_map.110 = (bf16[12,512]{1,0:T(8,128)(2,1)}, bf16[12,512]{1,0:T(8,128)(2,1)}, bf16[512,1024]{1,0:T(8,128)(2,1)}, bf16[1024,512]{1,0:T(8,128)(2,1)}, f32[64,512]{1,0:T(8,128)}) custom-call(bf16[12,512]{1,0:T(8,128)(2,1)} %x_ref.1, bf16[12,512]{1,0:T(8,128)(2,1)} %cot_ref.1, f32[1,512]{1,0:T(1,128)} %bitcast.15, bf16[64,512]{1,0:T(8,128)(2,1)} %bitcast.13, ...), custom_call_target="tpu_custom_call" | custom-call | flops 6000000000 | bytes 5242880 | tf_op jit(solution)/shard_map/pallas_call | solution.py:529
  225.0 0.0 copy-start.2
  225.0 1.3 copy.17
  226.4 0.0 copy-done.2
  226.4 0.6 copy.18
  227.0 0.0 copy-start
  227.0 2.4 %copy.19 = bf16[1,512,1024]{2,1,0:T(8,128)(2,1)} copy(bf16[1,512,1024]{2,1,0:T(8,128)(2,1)} %bitcast.9) | data formatting | bytes 2097152
  229.3 0.0 copy-done
  229.3 0.0 copy-start.1
  229.3 1.0 copy.20
  230.3 0.1 copy-done.1
  230.3 0.7 copy.21
Async XLA Ops:
  225.0 1.3 copy-start.2
  227.0 2.4 %copy-start = (bf16[1024,512]{1,0:T(8,128)(2,1)S(1)}, bf16[1024,512]{1,0:T(8,128)(2,1)}, u32[]{:S(2)}) copy-start(bf16[1024,512]{1,0:T(8,128)(2,1)} %get-tuple-element.13) | copy-start | bytes 3145732
  229.3 1.0 copy-start.1

commit v3 on v2

--- a/solution.py
+++ b/solution.py
@@ -9,22 +9,19 @@
 from jax.sharding import PartitionSpec as P
 
 EPSILON = 1e-06
-HIGHEST = lax.Precision.HIGHEST
 MESH = pl.DeviceIdType.MESH
 BF, F32 = jnp.bfloat16, jnp.float32
 PAD = 16
 MARKS = 64
-CHUNKS = 2
+CHUNKS = 3
 
 
 def iota(shape, dim):
     return lax.broadcasted_iota(jnp.int32, shape, dim)
 
 
-def dot(a, b, ca, cb, precision=None):
-    return lax.dot_general(
-        a, b, (((ca,), (cb,)), ((), ())), precision=precision, preferred_element_type=F32
-    )
+def dot(a, b, ca, cb):
+    return lax.dot_general(a, b, (((ca,), (cb,)), ((), ())), preferred_element_type=F32)
 
 
 def column(lanes):
@@ -38,8 +35,9 @@
 
 def kernel(
     s,
-    x_ref, cot_ref, gain_ref, sel_ref, up_ref, down_ref, routes_ref,
-    mixed_ref, dtok_ref, dup_ref, ddown_ref, dsel_ref,
+    x_ref, cot_ref, gain_ref, sel_ref, up_hbm, down_hbm, routes_ref,
+    mixed_ref, dtok_ref, dup_hbm, ddown_hbm, dsel_ref,
+    up_ref, down_ref, dup_ref, ddown_ref, own_sem,
     ax, ac, a1, a2, asel,
     pbuf, nbuf, qbuf, rbuf, full, ebuf,
     sb, sib, tb, rb, ub, zb,
@@ -81,6 +79,9 @@
     def each(count, fn):
         lax.fori_loop(1, count, lambda i, t: (fn(i), t)[1], 0)
 
+    def arrived(ref, sem):
+        pltpu.make_async_copy(ref, ref, sem).wait()
+
     pending = []
 
     def settle():
@@ -88,6 +89,12 @@
             drain()
         pending.clear()
 
+    up_in = pltpu.make_async_copy(up_hbm, up_ref, own_sem.at[0])
+    down_in = pltpu.make_async_copy(down_hbm, down_ref, own_sem.at[1])
+    dup_out = pltpu.make_async_copy(dup_ref, dup_hbm, own_sem.at[2])
+    ddown_out = pltpu.make_async_copy(ddown_ref, ddown_hbm, own_sem.at[3])
+    up_in.start()
+    down_in.start()
     barrier = pltpu.get_barrier_semaphore()
 
     def greet(device):
@@ -101,23 +108,14 @@
 
     def ag_hop(k, a, wave, i):
         src = a.at[c, q, zh if wave == 0 else 1 - zh]
-        return copy(src, src, ag_send.at[k, wave, i], ag_recv.at[k, wave, i], place(chip(i), zh, c))
+        return copy(src, src, ag_send.at[k, wave], ag_recv.at[k, wave], place(chip(i), zh, c))
 
     def ag_far(k, a):
         src = a.at[c, q, zh]
         return copy(src, src, az_send.at[k], az_recv.at[k], far)
 
-    def ag_twin(k, a, i):
-        src = a.at[c, lax.rem(q + Q - i, Q)]
-        return copy(src, src, as_send.at[k, i], as_recv.at[k, i], twin)
-
-    def ag_twin_wait(k, a):
-        ag_twin(k, a, 0).wait_recv()
-        each(Q, lambda i: ag_twin(k, a, i).wait_recv())
-
-    def ag_twin_drain(k, a):
-        ag_twin(k, a, 0).wait_send()
-        each(Q, lambda i: ag_twin(k, a, i).wait_send())
+    def ag_twin(k, a):
+        return copy(a.at[c], a.at[c], as_send.at[k], as_recv.at[k], twin)
 
     def ag_start(k, a):
         ag_far(k, a).start()
@@ -126,48 +124,40 @@
     def ag_forward(k, a):
         ag_far(k, a).wait_recv()
         each(Q, lambda i: ag_hop(k, a, 1, i).start())
-        ag_twin(k, a, 0).start()
+
+    def ag_join(k, a):
+        arrived(a.at[c, pl.ds(0, Q - 1), 0], ag_recv.at[k, 0])
+        arrived(a.at[c, pl.ds(0, Q - 1), 1], ag_recv.at[k, 1])
+        ag_twin(k, a).start()
+
+    def ag_finish(k, a):
+        ag_twin(k, a).wait_recv()
+
+        def drain():
+            ag_far(k, a).wait_send()
+            arrived(a.at[c, pl.ds(0, Q - 1), 0], ag_send.at[k, 0])
+            arrived(a.at[c, pl.ds(0, Q - 1), 1], ag_send.at[k, 1])
+            ag_twin(k, a).wait_send()
+
+        pending.append(drain)
 
     def ag_pair_hop(k, a, i):
         src = a.at[c, q]
-        return copy(src, src, ag_send.at[k, 0, i], ag_recv.at[k, 0, i], place(chip(i), zh, c))
+        return copy(src, src, ag_send.at[k, 0], ag_recv.at[k, 0], place(chip(i), zh, c))
 
     def ag_pair(k, a):
         each(Q, lambda i: ag_pair_hop(k, a, i).start())
-        ag_twin(k, a, 0).start()
 
     def ag_pair_join(k, a):
-        def pass_on(i):
-            ag_pair_hop(k, a, i).wait_recv()
-            ag_twin(k, a, i).start()
-
-        each(Q, pass_on)
+        arrived(a.at[c, pl.ds(0, Q - 1)], ag_recv.at[k, 0])
+        ag_twin(k, a).start()
 
     def ag_pair_finish(k, a):
-        ag_twin_wait(k, a)
+        ag_twin(k, a).wait_recv()
 
         def drain():
-            each(Q, lambda i: ag_pair_hop(k, a, i).wait_send())
-            ag_twin_drain(k, a)
-
-        pending.append(drain)
-
-    def ag_join(k, a):
-        def pass_on(i):
-            ag_hop(k, a, 0, i).wait_recv()
-            ag_hop(k, a, 1, i).wait_recv()
-            ag_twin(k, a, i).start()
-
-        each(Q, pass_on)
-
-    def ag_finish(k, a):
-        ag_twin_wait(k, a)
-
-        def drain():
-            ag_far(k, a).wait_send()
-            each(Q, lambda i: ag_hop(k, a, 0, i).wait_send())
-            each(Q, lambda i: ag_hop(k, a, 1, i).wait_send())
-            ag_twin_drain(k, a)
+            arrived(a.at[c, pl.ds(0, Q - 1)], ag_send.at[k, 0])
+            ag_twin(k, a).wait_send()
 
         pending.append(drain)
 
@@ -177,10 +167,10 @@
 
     def fs_hop(k, p, i):
         src, dst = qbuf.at[k, p, quad(i)], rbuf.at[k, p, i]
-        return copy(src, dst, fs_send.at[k, p, i], fs_recv.at[k, p, i], (e, 2 * quad(i) + par))
+        return copy(src, dst, fs_send.at[k, p], fs_recv.at[k, p], (e, 2 * quad(i) + par))
 
     def fs_ext(k, i):
-        return copy(ebuf.at[k, 0], ebuf.at[k, i], fx_send.at[k, i], fx_recv.at[k, i], (e, line(i)))
+        return copy(ebuf.at[k, 0], ebuf.at[k, i], fx_send.at[k], fx_recv.at[k], (e, line(i)))
 
     def fs_fill(k, part_of):
         for p in range(CHUNKS):
@@ -198,32 +188,32 @@
         def drain():
             for p in range(CHUNKS):
                 fs_near(k, p).wait_send()
-                each(F // 2, lambda i: fs_hop(k, p, i).wait_send())
+                arrived(rbuf.at[k, p, pl.ds(1, F // 2 - 1)], fs_send.at[k, p])
 
         pending.append(drain)
 
     def fs_sum(k, p):
+        arrived(rbuf.at[k, p, pl.ds(1, F // 2 - 1)], fs_recv.at[k, p])
         total = qbuf[k, p, m].astype(F32)
         for i in range(1, F // 2):
-            fs_hop(k, p, i).wait_recv()
             total = total + rbuf[k, p, i].astype(F32)
         return total
 
     def ext_start(k, value):
         ebuf[k, 0] = value
         each(F, lambda i: fs_ext(k, i).start())
-        pending.append(lambda: each(F, lambda i: fs_ext(k, i).wait_send()))
+        pending.append(lambda: arrived(ebuf.at[k, pl.ds(1, F - 1)], fx_send.at[k]))
 
     def ext_sum(k):
+        arrived(ebuf.at[k, pl.ds(1, F - 1)], fx_recv.at[k])
         total = ebuf[k, 0]
         for i in range(1, F):
-            fs_ext(k, i).wait_recv()
             total = total + ebuf[k, i]
         return total
 
     def fg_hop(k, p, i):
         src = full.at[k, p, par, m]
-        return copy(src, src, fs_send.at[4 + k, p, i], fs_recv.at[4 + k, p, i], (e, 2 * quad(i) + par))
+        return copy(src, src, fs_send.at[4 + k, p], fs_recv.at[4 + k, p], (e, 2 * quad(i) + par))
 
     def fg_near(k, p):
         src = full.at[k, p, par]
@@ -235,7 +225,7 @@
 
     def fg_forward(k):
         for p in range(CHUNKS):
-            each(F // 2, lambda i: fg_hop(k, p, i).wait_recv())
+            arrived(full.at[k, p, par, pl.ds(0, F // 2 - 1)], fs_recv.at[4 + k, p])
             fg_near(k, p).start()
 
     def fg_wait(k):
@@ -245,7 +235,7 @@
         def drain():
             for p in range(CHUNKS):
                 fg_near(k, p).wait_send()
-                each(F // 2, lambda i: fg_hop(k, p, i).wait_send())
+                arrived(full.at[k, p, par, pl.ds(0, F // 2 - 1)], fs_send.at[4 + k, p])
 
         pending.append(drain)
 
@@ -259,7 +249,7 @@
         return copy(sb.at[k], sib.at[k], rb_send.at[k], rb_recv.at[k], twin)
 
     def rs_hop(k, i):
-        return copy(tb.at[k, chip(i)], rb.at[k, i], rs_send.at[k, i], rs_recv.at[k, i], place(chip(i), zh, c))
+        return copy(tb.at[k, chip(i)], rb.at[k, i], rs_send.at[k], rs_recv.at[k], place(chip(i), zh, c))
 
     def rs_far(k):
         if k % 2:
@@ -278,9 +268,9 @@
         each(Q, lambda i: rs_hop(k, i).start())
 
     def rs_gather(k):
+        arrived(rb.at[k, pl.ds(1, Q - 1)], rs_recv.at[k])
         total = tb[k, q].astype(F32)
         for i in range(1, Q):
-            rs_hop(k, i).wait_recv()
             total = total + rb[k, i].astype(F32)
         ub[k] = total.astype(BF)
         rs_far(k).start()
@@ -290,7 +280,7 @@
 
         def drain():
             rs_twin(k).wait_send()
-            each(Q, lambda i: rs_hop(k, i).wait_send())
+            arrived(rb.at[k, pl.ds(1, Q - 1)], rs_send.at[k])
             rs_far(k).wait_send()
 
         pending.append(drain)
@@ -355,8 +345,8 @@
         y = xr * gain
         yb = y.astype(BF)
         fs_fill(loop, lambda part: dot(yb[part], up_ref[...], 1, 0))
-        squares = dot(jnp.ones((8, W), F32), xr * xr, 1, 1, HIGHEST)
-        logits = dot(sel_row, y, 1, 1, HIGHEST)
+        squares = dot(jnp.ones((8, W), BF), (xr * xr).astype(BF), 1, 1)
+        logits = dot(sel_row.astype(BF), yb, 1, 1)
         ext_start(loop, two_rows(squares, logits))
 
     def forward_mid(loop):
@@ -400,9 +390,9 @@
     def backward_ext(loop, st):
         dh = dh_k[loop]
         hg = (st.gate * dh * slope_k[loop]).astype(BF)
-        ones = jnp.ones((8, HL), F32)
-        gg = dot(ones, hid_k[loop].astype(F32) * dh, 1, 1, HIGHEST)
-        inner = dot(ones, hg.astype(F32) * pre_k[loop], 1, 1, HIGHEST)
+        ones = jnp.ones((8, HL), BF)
+        gg = dot(ones, (hid_k[loop].astype(F32) * dh).astype(BF), 1, 1)
+        inner = dot(ones, (hg.astype(F32) * pre_k[loop]).astype(BF), 1, 1)
         ext_start(2 + loop, two_rows(gg, inner))
 
     def backward_out(loop, st, k):
@@ -425,6 +415,7 @@
         return (grads[loop].astype(F32) * st.gate).astype(BF)
 
     build_gather(0)
+    up_in.wait()
     forward_in(0, ax)
     ag_start(1, ac)
     build_scatter(0)
@@ -437,6 +428,7 @@
     fg_forward(0)
     ag_finish(1, ac)
     fg_wait(0)
+    down_in.wait()
     forward_out(0, st0, 0)
     rs_spread(0)
     backward_in(1, ac)
@@ -463,7 +455,7 @@
     up_acc[...] = dot(n1, fg_value(3), 0, 0)
     fg_forward(1)
     rs_gather(2)
-    sel_acc = dot(jnp.broadcast_to(lgr1_l, (8, R)), n1.astype(F32), 1, 0, HIGHEST)
+    sel_acc = dot(jnp.broadcast_to(lgr1_l, (8, R)).astype(BF), n1, 1, 0)
     fg_wait(1)
     down_acc[...] = dot(fg_value(1), d_sent(1, st1), 0, 0)
     both = ac[c, q].astype(F32)
@@ -477,22 +469,24 @@
     rs_spread(1)
     fs_spread(2)
     ddown_ref[...] = (down_acc[...] + dot(fg_value(0), d_sent(0, st0), 0, 0)).astype(BF)
+    ddown_out.start()
     n0 = normed(0, st0)
     backward_mid(0, st0)
     backward_ext(0, st0)
     rs_gather(1)
     fg_forward(2)
     lgr0_l = backward_out(0, st0, 3)
-    sel_acc = sel_acc + dot(jnp.broadcast_to(lgr0_l, (8, R)), n0.astype(F32), 1, 0, HIGHEST)
+    rs_spread(3)
+    sel_acc = sel_acc + dot(jnp.broadcast_to(lgr0_l, (8, R)).astype(BF), n0, 1, 0)
     tile = jnp.zeros((8, 128), F32)
     for i in range(W // 128):
         tile = jnp.where(iota((8, 128), 0) == i, sel_acc[:, i * 128 : (i + 1) * 128], tile)
     asel[c, q, zh] = tile
     ag_start(4, asel)
-    rs_spread(3)
     settle()
     up0 = dot(n0, fg_value(2), 0, 0)
     dup_ref[...] = (up_acc[...] + up0).astype(BF)
+    dup_out.start()
     mixed_ref[...] = (a1[c, q, zh, 0:T].astype(F32) + rs_total(1)).astype(BF)
     ag_forward(4, asel)
     rs_gather(3)
@@ -502,6 +496,8 @@
         stack = asel[:, :, :, i, :].reshape(2, 2 * Q, 128)
         dsel_ref[:, i * 128 : (i + 1) * 128] = jnp.stack([stack[0], stack[1]], axis=1).reshape(4 * Q, 128)
     dtok_ref[...] = (a2[c, q, zh, 0:T].astype(F32) + rs_total(3)).astype(BF)
+    dup_out.wait()
+    ddown_out.wait()
     settle()
 
 
@@ -513,6 +509,7 @@
     half = Q * 2 * PAD
     gather = lambda w, t=BF, r=PAD: VM((2, Q, 2, r, w), t)
     scratch = [
+        VM((W, H), BF), VM((H, W), BF), VM((W, H), BF), VM((H, W), BF), DMA((4,)),
         gather(W + 2 * MARKS), gather(W), gather(W), gather(W), gather(128, F32, 8),
         VM((4, NC, 2, F // 2, RC, HL), BF), VM((4, NC, F // 2, RC, HL), BF), VM((4, NC, F // 2, RC, HL), BF),
         VM((4, NC, F // 2, RC, HL), BF), VM((4, NC, 2, F // 2, RC, HL), BF), VM((4, F, 8, R), F32),
@@ -521,11 +518,12 @@
         VM((2, R, 2 * half), BF), VM((2, 2, half, R), BF),
         VM((2, R, HL), F32), VM((2, R, HL), F32), VM((2, R, HL), BF), VM((2, R, HL), F32),
         VM((2, R, W), BF), VM((2, R, W), BF), VM((W, H), F32), VM((H, W), F32),
-        DMA((8, NC)), DMA((8, NC)), DMA((8, NC, F // 2)), DMA((8, NC, F // 2)), DMA((4, F)), DMA((4, F)),
-        DMA((5, 2, Q)), DMA((5, 2, Q)), DMA((5,)), DMA((5,)), DMA((5, Q)), DMA((5, Q)),
-        DMA((4, Q)), DMA((4, Q)), DMA((4,)), DMA((4,)), DMA((4,)), DMA((4,)),
+        DMA((8, NC)), DMA((8, NC)), DMA((8, NC)), DMA((8, NC)), DMA((4,)), DMA((4,)),
+        DMA((5, 2)), DMA((5, 2)), DMA((5,)), DMA((5,)), DMA((5,)), DMA((5,)),
+        DMA((4,)), DMA((4,)), DMA((4,)), DMA((4,)), DMA((4,)), DMA((4,)),
     ]
     T = tokens.shape[0]
+    vmem, hbm = pl.BlockSpec(memory_space=pltpu.VMEM), pl.BlockSpec(memory_space=pl.ANY)
     out = pl.pallas_call(
         functools.partial(kernel, s),
         out_shape=(
@@ -535,8 +533,8 @@
             jax.ShapeDtypeStruct((H, W), BF),
             jax.ShapeDtypeStruct((s.experts, W), F32),
         ),
-        in_specs=[pl.BlockSpec(memory_space=pltpu.VMEM)] * 7,
-        out_specs=[pl.BlockSpec(memory_space=pltpu.VMEM)] * 5,
+        in_specs=[vmem] * 4 + [hbm] * 2 + [vmem],
+        out_specs=[vmem] * 2 + [hbm] * 2 + [vmem],
         scratch_shapes=scratch,
         compiler_params=pltpu.CompilerParams(
             collective_id=0, has_side_effects=True, vmem_limit_bytes=60 * 1024 * 1024

time: 233 us -> 219 us (0.940)
  Pallas kernels: 224 us -> 211 us
    pallas_call x1, Pallas kernels: 224 us -> 211 us  [shards(): pl.pallas_call(functools.partial(kernel, s), out_shape=(jax.ShapeDtypeStr...]
where the time goes in v3:
time: 219 us; the launch traced here: 217 us
  Pallas kernels  211 us (96%)
  local copies, waits for them, and re-layouts  5.97 us (3%)
    pallas_call x1, Pallas kernels, shards(): pl.pallas_call(functools.partial(kernel, s), out_shape=(jax.ShapeDtypeStr...  211 us
    unnamed x11, local copies, waits for them, and re-layouts  5.97 us

profile of v3, /device:TPU:1, one launch (start us, length us, event | category | flops | bytes accessed | tf_op | source)
XLA Modules:
  0.0 217.2 jit_solution(14016595010639653119)
XLA Ops:
  0.6 210.6 %shard_map.110 = (bf16[12,512]{1,0:T(8,128)(2,1)}, bf16[12,512]{1,0:T(8,128)(2,1)}, bf16[512,1024]{1,0:T(8,128)(2,1)}, bf16[1024,512]{1,0:T(8,128)(2,1)}, f32[64,512]{1,0:T(8,128)}) custom-call(bf16[12,512]{1,0:T(8,128)(2,1)} %x_ref.1, bf16[12,512]{1,0:T(8,128)(2,1)} %cot_ref.1, f32[1,512]{1,0:T(1,128)} %bitcast.15, bf16[64,512]{1,0:T(8,128)(2,1)} %bitcast.13, ...), custom_call_target="tpu_custom_call" | custom-call | flops 6000000000 | bytes 5242880 | tf_op jit(solution)/shard_map/pallas_call | solution.py:527
  211.2 0.0 copy-start.2
  211.2 1.3 copy.17
  212.5 0.0 copy-done.2
  212.5 0.6 copy.18
  213.2 0.0 copy-start
  213.2 2.4 %copy.19 = bf16[1,512,1024]{2,1,0:T(8,128)(2,1)} copy(bf16[1,512,1024]{2,1,0:T(8,128)(2,1)} %bitcast.9) | data formatting | bytes 2097152
  215.5 0.0 copy-done
  215.5 0.0 copy-start.1
  215.5 1.0 copy.20
  216.5 0.1 copy-done.1
  216.5 0.7 copy.21
Async XLA Ops:
  211.2 1.3 copy-start.2
  213.2 2.4 %copy-start = (bf16[1024,512]{1,0:T(8,128)(2,1)S(1)}, bf16[1024,512]{1,0:T(8,128)(2,1)}, u32[]{:S(2)}) copy-start(bf16[1024,512]{1,0:T(8,128)(2,1)} %get-tuple-element.13) | copy-start | bytes 3145732
  215.5 1.0 copy-start.1

commit v4 on v3

--- a/solution.py
+++ b/solution.py
@@ -13,7 +13,7 @@
 BF, F32 = jnp.bfloat16, jnp.float32
 PAD = 16
 MARKS = 64
-CHUNKS = 3
+CHUNKS = 4
 
 
 def iota(shape, dim):

time: 219 us -> 214 us (0.977)
  Pallas kernels: 211 us -> 207 us
    pallas_call x1, Pallas kernels: 211 us -> 207 us  [shards(): pl.pallas_call(functools.partial(kernel, s), out_shape=(jax.ShapeDtypeStr...]
where the time goes in v4:
time: 214 us
  Pallas kernels  207 us (97%)
  local copies, waits for them, and re-layouts  5.97 us (3%)
    pallas_call x1, Pallas kernels, shards(): pl.pallas_call(functools.partial(kernel, s), out_shape=(jax.ShapeDtypeStr...  207 us
    unnamed x11, local copies, waits for them, and re-layouts  5.97 us

profile of v4, /device:TPU:1, one launch (start us, length us, event | category | flops | bytes accessed | tf_op | source)
XLA Modules:
  0.0 213.9 jit_solution(9540622176587305753)
XLA Ops:
  0.6 207.3 %shard_map.110 = (bf16[12,512]{1,0:T(8,128)(2,1)}, bf16[12,512]{1,0:T(8,128)(2,1)}, bf16[512,1024]{1,0:T(8,128)(2,1)}, bf16[1024,512]{1,0:T(8,128)(2,1)}, f32[64,512]{1,0:T(8,128)}) custom-call(bf16[12,512]{1,0:T(8,128)(2,1)} %x_ref.1, bf16[12,512]{1,0:T(8,128)(2,1)} %cot_ref.1, f32[1,512]{1,0:T(1,128)} %bitcast.15, bf16[64,512]{1,0:T(8,128)(2,1)} %bitcast.13, ...), custom_call_target="tpu_custom_call" | custom-call | flops 6000000000 | bytes 5242880 | tf_op jit(solution)/shard_map/pallas_call | solution.py:527
  207.9 0.0 copy-start.2
  207.9 1.3 copy.17
  209.2 0.0 copy-done.2
  209.2 0.6 copy.18
  209.8 0.0 copy-start
  209.8 2.4 %copy.19 = bf16[1,512,1024]{2,1,0:T(8,128)(2,1)} copy(bf16[1,512,1024]{2,1,0:T(8,128)(2,1)} %bitcast.9) | data formatting | bytes 2097152
  212.2 0.0 copy-done
  212.2 0.0 copy-start.1
  212.2 1.0 copy.20
  213.2 0.1 copy-done.1
  213.2 0.7 copy.21
Async XLA Ops:
  207.9 1.3 copy-start.2
  209.8 2.4 %copy-start = (bf16[1024,512]{1,0:T(8,128)(2,1)S(1)}, bf16[1024,512]{1,0:T(8,128)(2,1)}, u32[]{:S(2)}) copy-start(bf16[1024,512]{1,0:T(8,128)(2,1)} %get-tuple-element.13) | copy-start | bytes 3145732
  212.2 1.0 copy-start.1
